TPU v7x, 128 devices: a whole 4x4x4 slice. The times are simulated.
128 devices in a mesh: seq: 128 (over z, x, y, core).
Axes of the slice: x: 4, y: 4, z: 4, core: 2. Of those that a mesh axis runs over, the one named last changes fastest.
Arguments:
- hidden: bfloat16 [65536, 2560], P('seq'), may hold values from -6 to 6
- w_bc: bfloat16 [2560, 256], replicated, may hold values from -0.009765625 to 0.009765625
- ssm_in: bfloat16 [65536, 2560], P('seq'), may hold values from -6 to 6
- codes: int32 [40, 65536], P(None, 'seq'), may hold values from 0 to 2000, as said below
- rates: float32 [40], replicated, as said below
- skip: float32 [40], replicated, may hold values from 0.5 to 1.5
- grad_out: bfloat16 [65536, 2560], P('seq'), may hold values from -6 to 6
Outputs:
- mixed: bfloat16 [65536, 2560], P('seq')
- grad_x: bfloat16 [65536, 2560], P('seq')
- grad_w: float32 [2560, 256], replicated
Inputs may be any that keep to these rules, and one draw needn't show every extreme that they name: Decay codes; codes above 1000 mark sudden losses of state. Positive decay rates.
All inputs are finite; a program needn't handle non-finite values.
Results may differ from a plain program's by a relative error of at most 0.011.
Values sent between devices are 32-bit elements; how exact they have to be, the bound alone decides.
No kernel may reach another device: no remote copies, remote signals or barrier semaphores. Data moves between devices by JAX's collectives and lax.ppermute only.
A program may use at most 704 MiB of HBM per device.

v0:
```python
import functools

import jax
import jax.numpy as jnp
from jax import lax
from jax.experimental import pallas as pl
from jax.experimental.pallas import tpu as pltpu
from jax.sharding import Mesh
from jax.sharding import PartitionSpec as P

F32 = jnp.float32
BF16 = jnp.bfloat16
CHIP_AXES = ("z", "x", "y")
ALL_AXES = ("z", "x", "y", "c")
T = 512
H = 40
PS = 64
N = 128
D = 2560
G = 4
GH = H // G
GL = GH * PS
GT = GL // 128
NM = N // 8
CHIPS = 64
STATE_ROWS = 8 * GT
ROWS = 48
HALF_D = D // 2
GW_ROWS = 40
LARGE = 56 << 20
SMALL = 10 << 20
WHOLE = pl.BlockSpec(memory_space=pltpu.VMEM)


def mm(a, b):
    return jnp.dot(a, b, preferred_element_type=F32)


def mm_nt(a, b):
    return lax.dot_general(a, b, (((1,), (1,)), ((), ())), preferred_element_type=F32)


def mm_tn(a, b):
    return lax.dot_general(a, b, (((0,), (0,)), ((), ())), preferred_element_type=F32)


def spread_matrix():
    k = lax.broadcasted_iota(jnp.int32, (128, GL), 0)
    col = lax.broadcasted_iota(jnp.int32, (128, GL), 1)
    return jnp.where((k & 63) == (col >> 6), 1.0, 0.0).astype(BF16)


def spread(v, onehot):
    high = v.astype(BF16).astype(F32)
    low = pltpu.roll(v - high, 64, 1)
    lane = lax.broadcasted_iota(jnp.int32, v.shape, 1)
    return mm(jnp.where(lane < 64, high, low).astype(BF16), onehot)


def token_spec():
    return pl.BlockSpec((8, 128), lambda *_: (0, 0))


def token_shape():
    return jax.ShapeDtypeStruct((8, 128), F32)


def pre_kernel(
    c_ref, hidden_hbm, w_hbm, x_hbm, dy_hbm, codes_ref, rates_ref,
    bc_ref, cum_ref, cumt_ref, mine_hbm, other_hbm,
    hidden_scr, w_scr, x_scr, dy_scr, mine_scr, other_scr, group_scr, in_sem, out_sem,
):
    is_first = c_ref[0] == 0
    cols = [pl.ds(GL * q, GL) for q in range(G)]
    slices = [pl.ds(NM * q, NM) for q in range(G)]
    loads = []
    for q in range(G):
        for n, (src, dst) in enumerate(
            (
                (hidden_hbm.at[:, cols[q]], hidden_scr.at[q]),
                (w_hbm.at[cols[q], :], w_scr.at[q]),
                (x_hbm.at[:, cols[q]], x_scr.at[q]),
                (dy_hbm.at[:, cols[q]], dy_scr.at[q]),
            )
        ):
            loads.append(pltpu.make_async_copy(src, dst, in_sem.at[n, q]))
    for pick in ((0, 1), (2, 3)):
        for q in range(G):
            for n in pick:
                loads[4 * q + n].start()

    eye = lax.broadcasted_iota(jnp.int32, (H, H), 0) == lax.broadcasted_iota(
        jnp.int32, (H, H), 1
    )
    rates = jnp.sum(jnp.where(eye, rates_ref[...], 0.0), axis=1, keepdims=True)
    code = codes_ref[...].astype(F32)
    step = -(
        rates * jnp.minimum(code, 1000.0) / 1000.0
        + 0.0005 * jnp.maximum(code - 1000.0, 0.0)
    )
    s_at = lax.broadcasted_iota(jnp.int32, (T, T), 0)
    t_at = lax.broadcasted_iota(jnp.int32, (T, T), 1)
    upper = jnp.where(s_at <= t_at, 1.0, 0.0).astype(BF16)
    p1 = step.astype(BF16)
    rest = step - p1.astype(F32)
    p2 = rest.astype(BF16)
    p3 = (rest - p2.astype(F32)).astype(BF16)
    cum = mm(p1, upper) + mm(p2, upper) + mm(p3, upper)
    group_scr[...] = jnp.zeros_like(group_scr)
    onehot = spread_matrix()
    for q in range(G):
        group_scr[q, 0:GH, :] = cum[GH * q : GH * (q + 1), :]
        cum_ref[q] = group_scr[q, 0:16, :]
        cumt_ref[q] = group_scr[q].T

    acc = None
    for q in range(G):
        loads[4 * q].wait()
        loads[4 * q + 1].wait()
        part = mm(hidden_scr[q], w_scr[q])
        acc = part if acc is None else acc + part
    bc_ref[...] = acc.astype(BF16)

    stores = []
    for q in range(G):
        cumt = cumt_ref[q]
        fw = spread(jnp.exp(cumt), onehot)
        bw = spread(jnp.exp(cumt[T - 1 : T, :] - cumt), onehot)
        loads[4 * q + 2].wait()
        wi = (x_scr[q].astype(F32) * bw).astype(BF16)
        loads[4 * q + 3].wait()
        wg = (dy_scr[q].astype(F32) * fw).astype(BF16)
        sf = mm_tn(bc_ref[:, :N], wi)
        sb = mm_tn(bc_ref[:, N:], wg)
        decay = fw[T - 1 : T, :]
        for n, (scr, hbm, state) in enumerate(
            (
                (other_scr, other_hbm, jnp.where(is_first, sb, sf)),
                (mine_scr, mine_hbm, jnp.where(is_first, sf, sb)),
            )
        ):
            for m in range(NM):
                for i in range(GT):
                    lanes = slice(128 * i, 128 * i + 128)
                    scr[NM * q + m, 8 * i : 8 * i + 8, :] = state[8 * m : 8 * m + 8, lanes]
                    row = STATE_ROWS + i
                    scr[NM * q + m, row : row + 1, :] = decay[:, lanes]
                scr[NM * q + m, STATE_ROWS + GT : ROWS, :] = jnp.zeros(
                    (ROWS - STATE_ROWS - GT, 128), F32
                )
            stores.append(
                pltpu.make_async_copy(
                    scr.at[slices[q]], hbm.at[slices[q]], out_sem.at[n, q]
                )
            )
            stores[-1].start()
    for store in stores:
        store.wait()


def pre(core, hidden, w_bc, x, dy, codes, rates):
    hbm = pl.BlockSpec(memory_space=pl.ANY)
    return pl.pallas_call(
        pre_kernel,
        in_specs=[pl.BlockSpec(memory_space=pltpu.SMEM)] + [hbm] * 4 + [WHOLE] * 2,
        out_specs=[WHOLE] * 3 + [hbm] * 2,
        out_shape=[
            jax.ShapeDtypeStruct((T, 2 * N), BF16),
            jax.ShapeDtypeStruct((G, 16, T), F32),
            jax.ShapeDtypeStruct((G, T, 128), F32),
            jax.ShapeDtypeStruct((CHIPS, ROWS, 128), F32),
            jax.ShapeDtypeStruct((CHIPS, ROWS, 128), F32),
        ],
        scratch_shapes=[
            pltpu.VMEM((G, T, GL), BF16),
            pltpu.VMEM((G, GL, 2 * N), BF16),
            pltpu.VMEM((G, T, GL), BF16),
            pltpu.VMEM((G, T, GL), BF16),
            pltpu.VMEM((CHIPS, ROWS, 128), F32),
            pltpu.VMEM((CHIPS, ROWS, 128), F32),
            pltpu.VMEM((G, 128, T), F32),
            pltpu.SemaphoreType.DMA((4, G)),
            pltpu.SemaphoreType.DMA((2, G)),
        ],
        compiler_params=pltpu.CompilerParams(vmem_limit_bytes=LARGE),
        cost_estimate=pl.CostEstimate(
            flops=2 * 10**9, bytes_accessed=13 * 10**6, transcendentals=0
        ),
        name="pre",
    )(core, hidden, w_bc, x, dy, codes, rates)


def chip_kernel(mine_ref, got_ref, out_ref, token_ref):
    for m in range(CHIPS):
        for i in range(GT):
            other = got_ref[m, STATE_ROWS + i : STATE_ROWS + i + 1, :]
            rows = slice(8 * i, 8 * i + 8)
            out_ref[m, rows, :] = other * mine_ref[m, rows, :] + got_ref[m, rows, :]
        tail = slice(STATE_ROWS, ROWS)
        out_ref[m, tail, :] = mine_ref[m, tail, :] * got_ref[m, tail, :]
    token_ref[...] = jnp.zeros_like(token_ref)


def chip_sum(mine, got):
    return pl.pallas_call(
        chip_kernel,
        in_specs=[WHOLE, WHOLE],
        out_specs=[WHOLE, WHOLE],
        out_shape=[jax.ShapeDtypeStruct((CHIPS, ROWS, 128), F32), token_shape()],
        compiler_params=pltpu.CompilerParams(vmem_limit_bytes=SMALL),
        name="chip_sum",
    )(mine, got)


def scan_kernel(c_ref, in_ref, token_ref, out_ref):
    core = c_ref[0]
    state = [jnp.zeros((8, 128), F32) for _ in range(GT)]
    for k in range(CHIPS):
        at = k + core * (CHIPS - 1 - 2 * k)
        for i in range(GT):
            rows = slice(8 * i, 8 * i + 8)
            out_ref[at, rows, :] = state[i]
            decay = in_ref[at, STATE_ROWS + i : STATE_ROWS + i + 1, :]
            state[i] = decay * state[i] + in_ref[at, rows, :]


def scan_chips(core, slices, token):
    return pl.pallas_call(
        scan_kernel,
        in_specs=[pl.BlockSpec(memory_space=pltpu.SMEM), WHOLE, WHOLE],
        out_specs=WHOLE,
        out_shape=jax.ShapeDtypeStruct((CHIPS, STATE_ROWS, 128), F32),
        compiler_params=pltpu.CompilerParams(vmem_limit_bytes=SMALL),
        name="scan_chips",
    )(core, slices, token)


SPANS = ((0, 256), (0, 128), (256, 128))
CHUNK = 128


def span_weights(cumt, onehot, start, size):
    lo = slice(start, start + size)
    hi = slice(start + size, start + 2 * size)
    edge = cumt[start + size - 1 : start + size, :]
    u_lo = spread(jnp.exp(edge - cumt[lo, :]), onehot)
    u_hi = spread(jnp.exp(cumt[hi, :] - edge), onehot)
    return lo, hi, u_lo, u_hi


def chunk_masks():
    t_at = lax.broadcasted_iota(jnp.int32, (CHUNK, CHUNK), 0)
    s_at = lax.broadcasted_iota(jnp.int32, (CHUNK, CHUNK), 1)
    return t_at >= s_at, s_at < PS


def chunk_decay(cumt, cum_ref, rows, h, lower):
    gap = cumt[rows, h : h + 1] - cum_ref[0, h : h + 1, rows]
    return jnp.exp(jnp.where(lower, gap, -jnp.inf))


def pairs_kernel(
    c_ref, bc_ref, x_ref, dy_ref, cum_ref, cumt_ref, hidden_ref, after_ref,
    wmine_ref, wother_ref, dbc_ref, turned_ref, token_ref, kmat,
):
    q = pl.program_id(0)
    is_first = c_ref[0] == 0

    @pl.when(q == 0)
    def _():
        kmat[...] = jnp.zeros_like(kmat)

    turned_ref[...] = hidden_ref[...].T
    onehot = spread_matrix()
    cumt = cumt_ref[0]
    x = x_ref[...].astype(F32)
    dy = dy_ref[...].astype(F32)
    wg = dy * spread(jnp.exp(cumt), onehot)
    wi = x * spread(jnp.exp(cumt[T - 1 : T, :] - cumt), onehot)
    wmine_ref[...] = jnp.where(is_first, wg, wi).astype(BF16)
    wother_ref[...] = jnp.where(is_first, wi, wg).astype(BF16)
    for start, size in SPANS:
        lo, hi, u_lo, u_hi = span_weights(cumt, onehot, start, size)
        kmat[hi, lo] += mm_nt((dy[hi, :] * u_hi).astype(BF16), (x[lo, :] * u_lo).astype(BF16))
    lower, first = chunk_masks()
    for chunk in range(T // CHUNK):
        rows = slice(chunk * CHUNK, (chunk + 1) * CHUNK)
        ksum = jnp.zeros((CHUNK, CHUNK), F32)
        for i in range(GT):
            lanes = slice(128 * i, 128 * i + 128)
            xt = x_ref[rows, lanes]
            dyf = dy[rows, lanes]
            for e in range(2):
                own = first if e == 0 else jnp.logical_not(first)
                dyh = jnp.where(own, dyf, 0.0).astype(BF16)
                ksum += chunk_decay(cumt, cum_ref, rows, 2 * i + e, lower) * mm_nt(dyh, xt)
        kmat[rows, rows] += ksum

    @pl.when(q == G - 1)
    def _():
        k = kmat[...].astype(BF16)
        dbc_ref[:, :N] = mm_tn(k, bc_ref[:, N:])
        dbc_ref[:, N:] = mm(k, bc_ref[:, :N])
        token_ref[...] = jnp.zeros_like(token_ref)


def full_spec(*shape):
    return pl.BlockSpec(shape, lambda q: (0,) * len(shape))


def cols_spec(rows=T):
    return pl.BlockSpec((rows, GL), lambda q: (0, q))


def group_spec(*shape):
    return pl.BlockSpec((1, *shape), lambda q: (q, 0, 0))


def pairs(core, bc, x, dy, cum, cumt, hidden, token):
    return pl.pallas_call(
        pairs_kernel,
        grid=(G,),
        in_specs=[
            pl.BlockSpec(memory_space=pltpu.SMEM),
            full_spec(T, 2 * N),
            cols_spec(),
            cols_spec(),
            group_spec(16, T),
            group_spec(T, 128),
            cols_spec(),
            token_spec(),
        ],
        out_specs=[
            cols_spec(),
            cols_spec(),
            full_spec(T, 2 * N),
            pl.BlockSpec((GL, T), lambda q: (q, 0)),
            token_spec(),
        ],
        out_shape=[
            jax.ShapeDtypeStruct((T, D), BF16),
            jax.ShapeDtypeStruct((T, D), BF16),
            jax.ShapeDtypeStruct((T, 2 * N), F32),
            jax.ShapeDtypeStruct((D, T), BF16),
            token_shape(),
        ],
        scratch_shapes=[pltpu.VMEM((T, T), F32)],
        compiler_params=pltpu.CompilerParams(vmem_limit_bytes=LARGE),
        cost_estimate=pl.CostEstimate(
            flops=20 * 10**9, bytes_accessed=16 * 10**6, transcendentals=3 * 10**6
        ),
        name="pairs",
    )(core, bc, x, dy, cum, cumt, hidden, token)


def carry_kernel(w_ref, came_ref, acc_ref, state_ref):
    acc = jnp.zeros((T, N), F32)
    for q in range(G):
        for i in range(GT):
            rows = slice(8 * i, 8 * i + 8)
            lanes = slice(GL * q + 128 * i, GL * q + 128 * i + 128)
            for m in range(0, NM, 2):
                at = NM * q + m
                pair = jnp.concatenate([came_ref[at, rows, :], came_ref[at + 1, rows, :]])
                state_ref[8 * m : 8 * m + 16, lanes] = pair.astype(BF16)
        cols = slice(GL * q, GL * (q + 1))
        acc += mm_nt(w_ref[:, cols], state_ref[:, cols])
    acc_ref[...] = acc


def carry(w_mine, came):
    return pl.pallas_call(
        carry_kernel,
        in_specs=[WHOLE, WHOLE],
        out_specs=[WHOLE, WHOLE],
        out_shape=[
            jax.ShapeDtypeStruct((T, N), F32),
            jax.ShapeDtypeStruct((N, D), BF16),
        ],
        compiler_params=pltpu.CompilerParams(vmem_limit_bytes=SMALL),
        cost_estimate=pl.CostEstimate(
            flops=4 * 10**8, bytes_accessed=5 * 10**6, transcendentals=0
        ),
        name="carry",
    )(w_mine, came)


def weight_kernel(
    c_ref, accmine_ref, wother_ref, came_ref, theirs_ref, dbc_ref, turned_ref,
    gwmine_ref, gwother_ref, state_ref,
):
    core = c_ref[0]
    is_first = core == 0
    acc = jnp.zeros((T, N), F32)
    for q in range(G):
        for i in range(GT):
            rows = slice(8 * i, 8 * i + 8)
            lanes = slice(GL * q + 128 * i, GL * q + 128 * i + 128)
            tail = slice(STATE_ROWS + i, STATE_ROWS + i + 1)
            decay = theirs_ref[NM * q, tail, :]
            for m in range(0, NM, 2):
                at = NM * q + m
                pair = jnp.concatenate(
                    [
                        decay * came_ref[a, rows, :] + theirs_ref[a, rows, :]
                        for a in (at, at + 1)
                    ]
                )
                state_ref[8 * m : 8 * m + 16, lanes] = pair.astype(BF16)
        cols = slice(GL * q, GL * (q + 1))
        acc += mm_nt(wother_ref[:, cols], state_ref[:, cols])
    mine = accmine_ref[...]
    db = dbc_ref[:, :N] + jnp.where(is_first, acc, mine)
    dc = dbc_ref[:, N:] + jnp.where(is_first, mine, acc)
    dbc = (jnp.concatenate([db, dc], axis=1) * (1.0 / (T * 2 * CHIPS))).astype(BF16)
    for ref, half in ((gwother_ref, 1 - core), (gwmine_ref, core)):
        start = pl.multiple_of(half * HALF_D, HALF_D)
        part = mm(turned_ref[pl.ds(start, HALF_D), :], dbc)
        ref[0] = part[:, :N]
        ref[1] = part[:, N:]


def weight_part(core, acc_mine, w_other, came, theirs, dbc, turned):
    return pl.pallas_call(
        weight_kernel,
        in_specs=[pl.BlockSpec(memory_space=pltpu.SMEM)] + [WHOLE] * 6,
        out_specs=[WHOLE, WHOLE, WHOLE],
        out_shape=[
            jax.ShapeDtypeStruct((2, HALF_D, N), F32),
            jax.ShapeDtypeStruct((2, HALF_D, N), F32),
            jax.ShapeDtypeStruct((N, D), BF16),
        ],
        compiler_params=pltpu.CompilerParams(vmem_limit_bytes=20 << 20),
        cost_estimate=pl.CostEstimate(
            flops=2 * 10**9, bytes_accessed=12 * 10**6, transcendentals=0
        ),
        name="weight_part",
    )(core, acc_mine, w_other, came, theirs, dbc, turned)


def outputs_kernel(
    c_ref, bc_ref, x_ref, dy_ref, cum_ref, cumt_ref, skip_ref, smine_ref, sother_ref, after_ref,
    mixed_ref, gradx_ref, token_ref, scores, yacc, dxacc,
):
    is_first = c_ref[0] == 0
    b_mat = bc_ref[:, :N]
    c_mat = bc_ref[:, N:]

    @pl.when(pl.program_id(0) == 0)
    def _():
        scores[...] = mm_nt(c_mat, b_mat)

    onehot = spread_matrix()
    cumt = cumt_ref[0]
    x = x_ref[...].astype(F32)
    dy = dy_ref[...].astype(F32)
    skip = skip_ref[...]
    mine = smine_ref[...].astype(F32)
    other = sother_ref[...].astype(F32)
    s_prev = jnp.where(is_first, mine, other).astype(BF16)
    g_next = jnp.where(is_first, other, mine).astype(BF16)
    fw = spread(jnp.exp(cumt), onehot)
    yacc[...] = skip * x + fw * mm(c_mat, s_prev)
    bw = spread(jnp.exp(cumt[T - 1 : T, :] - cumt), onehot)
    dxacc[...] = skip * dy + bw * mm(b_mat, g_next)
    for start, size in SPANS:
        lo, hi, u_lo, u_hi = span_weights(cumt, onehot, start, size)
        pair = scores[hi, lo].astype(BF16)
        yacc[hi, :] += u_hi * mm(pair, (x[lo, :] * u_lo).astype(BF16))
        dxacc[lo, :] += u_lo * mm_tn(pair, (dy[hi, :] * u_hi).astype(BF16))
    lower, first = chunk_masks()
    for chunk in range(T // CHUNK):
        rows = slice(chunk * CHUNK, (chunk + 1) * CHUNK)
        score = scores[rows, rows]
        for i in range(GT):
            lanes = slice(128 * i, 128 * i + 128)
            xt = x_ref[rows, lanes]
            dyt = dy_ref[rows, lanes]
            ys, dxs = [], []
            for e in range(2):
                decay = chunk_decay(cumt, cum_ref, rows, 2 * i + e, lower)
                mixing = (score * decay).astype(BF16)
                ys.append(mm(mixing, xt))
                dxs.append(mm_tn(mixing, dyt))
            mixed_ref[rows, lanes] = (
                yacc[rows, lanes] + jnp.where(first, ys[0], ys[1])
            ).astype(BF16)
            gradx_ref[rows, lanes] = (
                dxacc[rows, lanes] + jnp.where(first, dxs[0], dxs[1])
            ).astype(BF16)
    token_ref[...] = jnp.zeros_like(token_ref)


def outputs(core, bc, x, dy, cum, cumt, skip_row, s_mine, s_other, token):
    return pl.pallas_call(
        outputs_kernel,
        grid=(G,),
        in_specs=[
            pl.BlockSpec(memory_space=pltpu.SMEM),
            full_spec(T, 2 * N),
            cols_spec(),
            cols_spec(),
            group_spec(16, T),
            group_spec(T, 128),
            cols_spec(1),
            cols_spec(N),
            cols_spec(N),
            token_spec(),
        ],
        out_specs=[cols_spec(), cols_spec(), token_spec()],
        out_shape=[
            jax.ShapeDtypeStruct((T, D), BF16),
            jax.ShapeDtypeStruct((T, D), BF16),
            token_shape(),
        ],
        scratch_shapes=[
            pltpu.VMEM((T, T), F32),
            pltpu.VMEM((T, GL), F32),
            pltpu.VMEM((T, GL), F32),
        ],
        compiler_params=pltpu.CompilerParams(vmem_limit_bytes=LARGE),
        cost_estimate=pl.CostEstimate(
            flops=25 * 10**9, bytes_accessed=13 * 10**6, transcendentals=3 * 10**6
        ),
        name="outputs",
    )(core, bc, x, dy, cum, cumt, skip_row, s_mine, s_other, token)


def add_kernel(a_ref, b_ref, out_ref, token_ref):
    out_ref[...] = a_ref[...] + b_ref[...]
    token_ref[...] = jnp.zeros_like(token_ref)


def pair_add(a, b):
    return pl.pallas_call(
        add_kernel,
        in_specs=[WHOLE, WHOLE],
        out_specs=[WHOLE, WHOLE],
        out_shape=[jax.ShapeDtypeStruct(a.shape, F32), token_shape()],
        compiler_params=pltpu.CompilerParams(vmem_limit_bytes=SMALL),
        name="pair_add",
    )(a, b)


def total_kernel(in_ref, token_ref, out_ref):
    total = jnp.sum(in_ref[...], axis=0)
    for k in range(CHIPS):
        out_ref[k] = total


def chip_total(parts, token):
    return pl.pallas_call(
        total_kernel,
        in_specs=[WHOLE, WHOLE],
        out_specs=WHOLE,
        out_shape=jax.ShapeDtypeStruct((CHIPS, GW_ROWS, 128), F32),
        compiler_params=pltpu.CompilerParams(vmem_limit_bytes=SMALL),
        name="chip_total",
    )(parts, token)


def place_kernel(c_ref, half_ref, *refs):
    out_ref = refs[-1]
    for lane in range(2):
        out_ref[:, 128 * lane : 128 * lane + 128] = half_ref[lane]


def place(at, half, into):
    block = HALF_D // 2
    extra = [] if into is None else [into]
    return pl.pallas_call(
        place_kernel,
        grid_spec=pltpu.PrefetchScalarGridSpec(
            num_scalar_prefetch=1,
            grid=(2,),
            in_specs=[pl.BlockSpec((2, block, 128), lambda i, c: (0, i, 0))]
            + [pl.BlockSpec(memory_space=pl.ANY)] * len(extra),
            out_specs=pl.BlockSpec((block, 2 * N), lambda i, c: (2 * c[0] + i, 0)),
        ),
        out_shape=jax.ShapeDtypeStruct((D, 2 * N), F32),
        input_output_aliases={2: 0} if extra else {},
        compiler_params=pltpu.CompilerParams(vmem_limit_bytes=SMALL),
        name="place",
    )(at, half, *extra)


def swap(v):
    return lax.ppermute(v, "c", [(0, 1), (1, 0)])


def exchange(v):
    return lax.all_to_all(v, CHIP_AXES, 0, 0, tiled=True)


def shards(hidden, w_bc, ssm_in, codes, rates, skip, grad_out):
    core = lax.axis_index("c").astype(jnp.int32).reshape(1)
    skip_row = jnp.repeat(skip, PS)[None, :]
    bc, cum, cumt, mine, other = pre(
        core, hidden, w_bc, ssm_in, grad_out, codes, rates[None, :]
    )
    chip, token = chip_sum(mine, swap(other))
    slices = exchange(chip)
    theirs = swap(mine)
    w_mine, w_other, dbc, turned, token = pairs(
        core, bc, ssm_in, grad_out, cum, cumt, hidden, token
    )
    came = exchange(scan_chips(core, slices, token))
    acc_mine, s_mine = carry(w_mine, came)
    gw_mine, gw_other, s_other = weight_part(
        core, acc_mine, w_other, swap(came), theirs, dbc, turned
    )
    part, token = pair_add(gw_mine, swap(gw_other))
    sums = exchange(part.reshape(CHIPS, GW_ROWS, 128))
    mixed, gradx, token = outputs(
        core, bc, ssm_in, grad_out, cum, cumt, skip_row, s_mine, s_other, token
    )
    half = exchange(chip_total(sums, token)).reshape(2, HALF_D, 128)
    grad_w = place(1 - core, swap(half), place(core, half, None))
    return mixed, gradx, grad_w


def solution(mesh):
    grid = Mesh(mesh.devices.reshape(4, 4, 4, 2), ALL_AXES)
    rows = P(ALL_AXES, None)
    return jax.shard_map(
        shards,
        mesh=grid,
        in_specs=(rows, P(), rows, P(None, ALL_AXES), P(), P(), rows),
        out_specs=(rows, rows, P()),
        check_vma=False,
    )
```

profile of v0, /device:TPU:1, one launch (start us, length us, event | category | flops | bytes accessed | tf_op | source)
XLA Modules:
  0.0 156.8 jit_solution(13722098838702497973)
XLA Ops:
  0.6 10.9 %pre.1 = (bf16[512,256]{1,0:T(8,128)(2,1)}, f32[4,16,512]{2,1,0:T(8,128)}, f32[4,512,128]{2,1,0:T(8,128)}, f32[64,48,128]{2,1,0:T(8,128)}, f32[64,48,128]{2,1,0:T(8,128)}) custom-call(s32[1]{0:T(128)} %bitcast.c_ref, bf16[512,2560]{1,0:T(8,128)(2,1)} %hidden_ref.1, bf16[2560,256]{1,0:T(8,128)(2,1)} %w_hbm.1, bf16[512,2560]{1,0:T(8,128)(2,1)} %x_ref.3, ...), custom_call_target="tpu_custom_call" | custom-call | flops 2000000000 | bytes 13000000 | tf_op jit(solution)/shard_map/pre/pallas_call | solution.py:163
  11.5 1.5 collective-permute-start
  13.0 3.2 %collective-permute-done.got_ref = f32[64,48,128]{2,1,0:T(8,128)S(1)} collective-permute-done((f32[64,48,128]{2,1,0:T(8,128)}, f32[64,48,128]{2,1,0:T(8,128)S(1)}, u32[]{:S(2)}, u32[]{:S(2)}) %collective-permute-start) | collective-permute-done | bytes 1572896 | tf_op jit(solution)/shard_map/ppermute | solution.py:588
  16.3 0.0 copy-start.3
  16.3 1.4 copy-done.3
  17.7 1.4 chip_sum.1
  19.0 0.0 copy-start.11
  19.0 0.6 copy-done.11
  19.6 11.2 %all-to-all-start = ((f32[64,48,128]{2,1,0:T(8,128)}), f32[64,48,128]{2,1,0:T(8,128)S(1)}, u32[]{:S(2)}, u32[]{:S(2)}) async-start(f32[64,48,128]{2,1,0:T(8,128)} %get-tuple-element.32), calls=%async_computation | async-start | bytes 3145728 | tf_op jit(solution)/shard_map/all_to_all | solution.py:592
  30.9 13.9 %pairs.1 = (bf16[512,2560]{1,0:T(8,128)(2,1)}, bf16[512,2560]{1,0:T(8,128)(2,1)}, f32[512,256]{1,0:T(8,128)}, bf16[2560,512]{1,0:T(8,128)(2,1)}, f32[8,128]{1,0:T(8,128)}) custom-call(s32[1]{0:T(128)} %bitcast.c_ref, bf16[512,256]{1,0:T(8,128)(2,1)} %get-tuple-element.25.bc_ref, bf16[512,2560]{1,0:T(8,128)(2,1)} %x_ref.3, bf16[512,2560]{1,0:T(8,128)(2,1)} %dy_ref.3, ...), custom_call_target="tpu_custom_call" | custom-call | flops 20000000000 | bytes 16000000 | tf_op jit(solution)/shard_map/pairs/pallas_call | solution.py:320
  44.8 8.9 %all-to-all-done.in_ref = f32[64,48,128]{2,1,0:T(8,128)S(1)} async-done(((f32[64,48,128]{2,1,0:T(8,128)}), f32[64,48,128]{2,1,0:T(8,128)S(1)}, u32[]{:S(2)}, u32[]{:S(2)}) %all-to-all-start) | async-done | bytes 1572896 | tf_op jit(solution)/shard_map/all_to_all | solution.py:592
  53.6 0.0 copy-start.7
  53.6 0.7 copy-done.7
  54.3 1.3 scan_chips.1
  55.6 5.5 %all-to-all-start.1 = ((f32[64,40,128]{2,1,0:T(8,128)}), f32[64,40,128]{2,1,0:T(8,128)S(1)}, u32[]{:S(2)}, u32[]{:S(2)}) async-start(f32[64,40,128]{2,1,0:T(8,128)} %scan_chips.1), calls=%async_computation.1 | async-start | bytes 2621440 | tf_op jit(solution)/shard_map/all_to_all | solution.py:592
  61.2 2.4 %collective-permute-start.2 = (f32[64,48,128]{2,1,0:T(8,128)}, f32[64,48,128]{2,1,0:T(8,128)S(1)}, u32[]{:S(2)}, u32[]{:S(2)}) collective-permute-start(f32[64,48,128]{2,1,0:T(8,128)} %get-tuple-element.28.mine_ref), channel_id=1, source_target_pairs={{0,1},{1,0},{2,3},{3,2},{4,5},{5,4},{6,7},{7,6},{8,9},{9,8},{10,11... | collective-permute-start | bytes 4718600 | tf_op jit(solution)/shard_map/ppermute | solution.py:588
  63.6 16.3 %all-to-all-done.1.came_ref = f32[64,40,128]{2,1,0:T(8,128)S(1)} async-done(((f32[64,40,128]{2,1,0:T(8,128)}), f32[64,40,128]{2,1,0:T(8,128)S(1)}, u32[]{:S(2)}, u32[]{:S(2)}) %all-to-all-start.1) | async-done | bytes 1310752 | tf_op jit(solution)/shard_map/all_to_all | solution.py:592
  79.9 3.7 %collective-permute-start.1 = (f32[64,40,128]{2,1,0:T(8,128)S(1)}, f32[64,40,128]{2,1,0:T(8,128)S(1)}, u32[]{:S(2)}, u32[]{:S(2)}) collective-permute-start(f32[64,40,128]{2,1,0:T(8,128)S(1)} %all-to-all-done.1.came_ref), channel_id=1, source_target_pairs={{0,1},{1,0},{2,3},{3,2},{4,5},{5,4},{6,7},{7,6},{8,9},{9,8},{10,11... | collective-permute-start | bytes 3932168 | tf_op jit(solution)/shard_map/ppermute | solution.py:588
  83.6 0.0 copy-start
  83.6 1.7 %copy-done = bf16[512,2560]{1,0:T(8,128)(2,1)S(1)} copy-done((bf16[512,2560]{1,0:T(8,128)(2,1)S(1)}, bf16[512,2560]{1,0:T(8,128)(2,1)}, u32[]{:S(2)}) %copy-start) | copy-done | bytes 2621464
  85.3 0.0 copy-start.1
  85.3 0.0 copy-start.5
  85.3 0.9 carry.1
  86.2 0.0 copy-start.8
  86.2 0.8 copy-done.8
  87.1 0.0 collective-permute-done.2.theirs_ref
  87.1 0.0 collective-permute-done.1.came_ref
  87.1 0.0 copy-done.1
  87.1 0.1 copy-done.5
  87.2 0.0 copy-start.2
  87.2 1.7 %copy-done.2 = bf16[2560,512]{1,0:T(8,128)(2,1)S(1)} copy-done((bf16[2560,512]{1,0:T(8,128)(2,1)S(1)}, bf16[2560,512]{1,0:T(8,128)(2,1)}, u32[]{:S(2)}) %copy-start.2) | copy-done | bytes 2621464
  89.0 0.0 copy-start.12
  89.0 2.8 %weight_part.1 = (f32[2,1280,128]{2,1,0:T(8,128)S(1)}, f32[2,1280,128]{2,1,0:T(8,128)}, bf16[128,2560]{1,0:T(8,128)(2,1)S(1)}) custom-call(s32[1]{0:T(128)} %bitcast.c_ref, f32[512,128]{1,0:T(8,128)S(1)} %get-tuple-element.35.accmine_ref, bf16[512,2560]{1,0:T(8,128)(2,1)S(1)} %copy-done.1, f32[64,40,128]{2,1,0:T(8,128)S(1)} %collective-permute-done.1.came_ref, ...), custom_call_target="tpu_custom_call" | custom-call | flops 2000000000 | bytes 12000000 | tf_op jit(solution)/shard_map/weight_part/pallas_call | solution.py:424
  91.8 0.0 copy-start.9
  91.8 0.8 copy-done.9
  92.6 0.0 collective-permute-start.3
  92.6 0.0 copy-done.12
  92.6 0.1 broadcast_in_dim.7
  92.7 0.7 broadcast_in_dim_reshape.3.skip_ref
  93.4 2.5 %collective-permute-done.3.b_ref = f32[2,1280,128]{2,1,0:T(8,128)S(1)} collective-permute-done((f32[2,1280,128]{2,1,0:T(8,128)}, f32[2,1280,128]{2,1,0:T(8,128)S(1)}, u32[]{:S(2)}, u32[]{:S(2)}) %collective-permute-start.3) | collective-permute-done | bytes 1310752 | tf_op jit(solution)/shard_map/ppermute | solution.py:588
  95.9 0.1 pair_add.1
  96.0 0.0 copy-start.4
  96.0 1.0 copy-done.4
  97.0 0.0 copy-start.10
  97.0 4.7 %all-to-all-start.2 = ((f32[64,40,128]{2,1,0:T(8,128)}), f32[64,40,128]{2,1,0:T(8,128)S(1)}, u32[]{:S(2)}, u32[]{:S(2)}) async-start(f32[64,40,128]{2,1,0:T(8,128)} %bitcast.6), calls=%async_computation.2 | async-start | bytes 2621440 | tf_op jit(solution)/shard_map/all_to_all | solution.py:592
  101.8 0.0 copy-done.10
  101.8 18.4 %outputs.1 = (bf16[512,2560]{1,0:T(8,128)(2,1)}, bf16[512,2560]{1,0:T(8,128)(2,1)}, f32[8,128]{1,0:T(8,128)}) custom-call(s32[1]{0:T(128)} %bitcast.c_ref, bf16[512,256]{1,0:T(8,128)(2,1)} %get-tuple-element.25.bc_ref, bf16[512,2560]{1,0:T(8,128)(2,1)} %x_ref.3, bf16[512,2560]{1,0:T(8,128)(2,1)} %dy_ref.3, f32[4,16,512]{2,1,0:T(8,128)} %get-tuple-element.26.cum_ref, ...), custom_call_target="tpu_custom_call" | custom-call | flops 24999999488 | bytes 13000000 | tf_op jit(solution)/shard_map/outputs/pallas_call | solution.py:495
  120.2 2.1 %all-to-all-done.2.in_ref = f32[64,40,128]{2,1,0:T(8,128)S(1)} async-done(((f32[64,40,128]{2,1,0:T(8,128)}), f32[64,40,128]{2,1,0:T(8,128)S(1)}, u32[]{:S(2)}, u32[]{:S(2)}) %all-to-all-start.2) | async-done | bytes 1310752 | tf_op jit(solution)/shard_map/all_to_all | solution.py:592
  122.3 0.0 copy-start.6
  122.3 0.7 copy-done.6
  123.0 0.2 chip_total.1
  123.1 27.2 %all_to_all.20 = f32[64,40,128]{2,1,0:T(8,128)S(1)} all-to-all(f32[64,40,128]{2,1,0:T(8,128)S(1)} %chip_total.1), channel_id=1, replica_groups=mesh['z'=4,'x'=4,'y'=4,'c'=2] {'z','x','y'}, dimensions={0} | all-to-all | bytes 2621440 | tf_op jit(solution)/shard_map/all_to_all | solution.py:592
  150.3 2.6 %collective-permute-start.4 = (f32[2,1280,128]{2,1,0:T(8,128)S(1)}, f32[2,1280,128]{2,1,0:T(8,128)S(1)}, u32[]{:S(2)}, u32[]{:S(2)}) collective-permute-start(f32[2,1280,128]{2,1,0:T(8,128)S(1)} %bitcast.4), channel_id=1, source_target_pairs={{0,1},{1,0},{2,3},{3,2},{4,5},{5,4},{6,7},{7,6},{8,9},{9,8},{10,11... | collective-permute-start | bytes 3932168 | tf_op jit(solution)/shard_map/ppermute | solution.py:588
  153.0 1.2 place.2.refs_0_
  154.2 1.5 collective-permute-done.4.half_ref
  155.6 1.2 place.3
Async XLA Ops:
  11.5 4.7 %collective-permute-start = (f32[64,48,128]{2,1,0:T(8,128)}, f32[64,48,128]{2,1,0:T(8,128)S(1)}, u32[]{:S(2)}, u32[]{:S(2)}) collective-permute-start(f32[64,48,128]{2,1,0:T(8,128)} %get-tuple-element.29), channel_id=1, source_target_pairs={{0,1},{1,0},{2,3},{3,2},{4,5},{5,4},{6,7},{7,6},{8,9},{9,8},{10,11... | collective-permute-start | bytes 4718600 | tf_op jit(solution)/shard_map/ppermute | solution.py:588
  16.3 1.4 copy-start.3
  19.0 0.6 copy-start.11
  19.6 34.0 %all-to-all-start = ((f32[64,48,128]{2,1,0:T(8,128)}), f32[64,48,128]{2,1,0:T(8,128)S(1)}, u32[]{:S(2)}, u32[]{:S(2)}) async-start(f32[64,48,128]{2,1,0:T(8,128)} %get-tuple-element.32), calls=%async_computation | async-start | bytes 3145728 | tf_op jit(solution)/shard_map/all_to_all | solution.py:592
  53.6 0.7 copy-start.7
  55.6 24.3 %all-to-all-start.1 = ((f32[64,40,128]{2,1,0:T(8,128)}), f32[64,40,128]{2,1,0:T(8,128)S(1)}, u32[]{:S(2)}, u32[]{:S(2)}) async-start(f32[64,40,128]{2,1,0:T(8,128)} %scan_chips.1), calls=%async_computation.1 | async-start | bytes 2621440 | tf_op jit(solution)/shard_map/all_to_all | solution.py:592
  61.2 25.9 %collective-permute-start.2 = (f32[64,48,128]{2,1,0:T(8,128)}, f32[64,48,128]{2,1,0:T(8,128)S(1)}, u32[]{:S(2)}, u32[]{:S(2)}) collective-permute-start(f32[64,48,128]{2,1,0:T(8,128)} %get-tuple-element.28.mine_ref), channel_id=1, source_target_pairs={{0,1},{1,0},{2,3},{3,2},{4,5},{5,4},{6,7},{7,6},{8,9},{9,8},{10,11... | collective-permute-start | bytes 4718600 | tf_op jit(solution)/shard_map/ppermute | solution.py:588
  79.9 7.2 %collective-permute-start.1 = (f32[64,40,128]{2,1,0:T(8,128)S(1)}, f32[64,40,128]{2,1,0:T(8,128)S(1)}, u32[]{:S(2)}, u32[]{:S(2)}) collective-permute-start(f32[64,40,128]{2,1,0:T(8,128)S(1)} %all-to-all-done.1.came_ref), channel_id=1, source_target_pairs={{0,1},{1,0},{2,3},{3,2},{4,5},{5,4},{6,7},{7,6},{8,9},{9,8},{10,11... | collective-permute-start | bytes 3932168 | tf_op jit(solution)/shard_map/ppermute | solution.py:588
  83.6 1.7 %copy-start = (bf16[512,2560]{1,0:T(8,128)(2,1)S(1)}, bf16[512,2560]{1,0:T(8,128)(2,1)}, u32[]{:S(2)}) copy-start(bf16[512,2560]{1,0:T(8,128)(2,1)} %get-tuple-element.31.w_ref) | copy-start | bytes 7864324
  85.3 1.8 %copy-start.1 = (bf16[512,2560]{1,0:T(8,128)(2,1)S(1)}, bf16[512,2560]{1,0:T(8,128)(2,1)}, u32[]{:S(2)}) copy-start(bf16[512,2560]{1,0:T(8,128)(2,1)} %get-tuple-element.36.wother_ref) | copy-start | bytes 7864324
  85.3 1.9 %copy-start.5 = (f32[512,256]{1,0:T(8,128)S(1)}, f32[512,256]{1,0:T(8,128)}, u32[]{:S(2)}) copy-start(f32[512,256]{1,0:T(8,128)} %get-tuple-element.37.dbc_ref) | copy-start | bytes 1572868
  86.2 0.8 copy-start.8
  87.2 1.7 %copy-start.2 = (bf16[2560,512]{1,0:T(8,128)(2,1)S(1)}, bf16[2560,512]{1,0:T(8,128)(2,1)}, u32[]{:S(2)}) copy-start(bf16[2560,512]{1,0:T(8,128)(2,1)} %get-tuple-element.38.turned_ref) | copy-start | bytes 7864324
  89.0 3.6 %copy-start.12 = (f32[40]{0:T(128)S(1)}, f32[40]{0:T(128)}, u32[]{:S(2)}) copy-start(f32[40]{0:T(128)} %param.12) | copy-start | bytes 484
  91.8 0.8 copy-start.9
  92.6 3.2 %collective-permute-start.3 = (f32[2,1280,128]{2,1,0:T(8,128)}, f32[2,1280,128]{2,1,0:T(8,128)S(1)}, u32[]{:S(2)}, u32[]{:S(2)}) collective-permute-start(f32[2,1280,128]{2,1,0:T(8,128)} %get-tuple-element.41), channel_id=1, source_target_pairs={{0,1},{1,0},{2,3},{3,2},{4,5},{5,4},{6,7},{7,6},{8,9},{9,8},{10,11... | collective-permute-start | bytes 3932168 | tf_op jit(solution)/shard_map/ppermute | solution.py:588
  96.0 1.1 copy-start.4
  97.0 4.7 %copy-start.10 = (f32[8,128]{1,0:T(8,128)}, f32[8,128]{1,0:T(8,128)S(1)}, u32[]{:S(2)}) copy-start(f32[8,128]{1,0:T(8,128)S(1)} %get-tuple-element.42.after_ref) | copy-start | bytes 12292
  97.0 25.2 %all-to-all-start.2 = ((f32[64,40,128]{2,1,0:T(8,128)}), f32[64,40,128]{2,1,0:T(8,128)S(1)}, u32[]{:S(2)}, u32[]{:S(2)}) async-start(f32[64,40,128]{2,1,0:T(8,128)} %bitcast.6), calls=%async_computation.2 | async-start | bytes 2621440 | tf_op jit(solution)/shard_map/all_to_all | solution.py:592
  122.3 0.7 copy-start.6
  150.3 5.3 %collective-permute-start.4 = (f32[2,1280,128]{2,1,0:T(8,128)S(1)}, f32[2,1280,128]{2,1,0:T(8,128)S(1)}, u32[]{:S(2)}, u32[]{:S(2)}) collective-permute-start(f32[2,1280,128]{2,1,0:T(8,128)S(1)} %bitcast.4), channel_id=1, source_target_pairs={{0,1},{1,0},{2,3},{3,2},{4,5},{5,4},{6,7},{7,6},{8,9},{9,8},{10,11... | collective-permute-start | bytes 3932168 | tf_op jit(solution)/shard_map/ppermute | solution.py:588
where the time goes:
time: 157 us
  Pallas kernels  52.2 us (33%)
  waiting for transfers between devices  34.4 us (22%)
  starting transfers between devices  31.8 us (20%)
  blocking collectives  27.2 us (17%)
  local copies, waits for them, and re-layouts  10.5 us (7%)
    all_to_all x3, waiting for transfers between devices, exchange(): return lax.all_to_all(v, CHIP_AXES, 0, 0, tiled=True)  27.3 us
    all_to_all x1, blocking collectives, exchange(): return lax.all_to_all(v, CHIP_AXES, 0, 0, tiled=True)  27.2 us
    all_to_all x3, starting transfers between devices, exchange(): return lax.all_to_all(v, CHIP_AXES, 0, 0, tiled=True)  21.5 us
    pallas_call x1, Pallas kernels, outputs(): pl.pallas_call(outputs_kernel, grid=(G,), in_specs=[pl.BlockSpec(memory_s...  18.4 us
    pallas_call x1, Pallas kernels, pairs(): pl.pallas_call(pairs_kernel, grid=(G,), in_specs=[pl.BlockSpec(memory_spa...  13.9 us
    pallas_call x1, Pallas kernels, pre(): pl.pallas_call(pre_kernel, in_specs=[pl.BlockSpec(memory_space=pltpu.SMEM...  10.9 us
    ppermute x5, starting transfers between devices, swap(): return lax.ppermute(v, 'c', [(0, 1), (1, 0)])  10.3 us
    unnamed x26, local copies, waits for them, and re-layouts  9.71 us
  transfers between devices with their start and end apart: 8, of which 6 were waited for; matrix products, arithmetic and copies ran while one was open for 0% of the time, Pallas kernels for 22%

commit v1 on v0

--- a/solution.py
+++ b/solution.py
@@ -27,9 +27,15 @@
 ROWS = 48
 HALF_D = D // 2
 GW_ROWS = 40
+KC = 5
+KL = D // KC
 LARGE = 56 << 20
+MIDDLE = 44 << 20
 SMALL = 10 << 20
 WHOLE = pl.BlockSpec(memory_space=pltpu.VMEM)
+IN_HBM = pl.BlockSpec(memory_space=pltpu.HBM)
+IN_SMEM = pl.BlockSpec(memory_space=pltpu.SMEM)
+TOKEN = jax.ShapeDtypeStruct((1,), jnp.int32)
 
 
 def mm(a, b):
@@ -57,82 +63,95 @@
     return mm(jnp.where(lane < 64, high, low).astype(BF16), onehot)
 
 
-def token_spec():
-    return pl.BlockSpec((8, 128), lambda *_: (0, 0))
-
-
-def token_shape():
-    return jax.ShapeDtypeStruct((8, 128), F32)
-
-
 def pre_kernel(
-    c_ref, hidden_hbm, w_hbm, x_hbm, dy_hbm, codes_ref, rates_ref,
-    bc_ref, cum_ref, cumt_ref, mine_hbm, other_hbm,
-    hidden_scr, w_scr, x_scr, dy_scr, mine_scr, other_scr, group_scr, in_sem, out_sem,
+    c_ref, rates_ref, hidden_hbm, w_hbm, x_hbm, dy_hbm, codes_hbm,
+    bc_hbm, cum_hbm, cumt_hbm, mine_hbm, other_hbm,
+    hidden_scr, w_scr, x_scr, dy_scr, codes_scr, bc_scr, cum_scr, cumt_scr, mine_scr, other_scr,
+    in_sem, out_sem, small_sem,
 ):
     is_first = c_ref[0] == 0
     cols = [pl.ds(GL * q, GL) for q in range(G)]
-    slices = [pl.ds(NM * q, NM) for q in range(G)]
-    loads = []
-    for q in range(G):
-        for n, (src, dst) in enumerate(
-            (
-                (hidden_hbm.at[:, cols[q]], hidden_scr.at[q]),
-                (w_hbm.at[cols[q], :], w_scr.at[q]),
-                (x_hbm.at[:, cols[q]], x_scr.at[q]),
-                (dy_hbm.at[:, cols[q]], dy_scr.at[q]),
+    code_load = pltpu.make_async_copy(codes_hbm, codes_scr, small_sem.at[0])
+    code_load.start()
+    loads = {}
+    for n, (src, dst) in enumerate(((x_hbm, x_scr), (dy_hbm, dy_scr))):
+        for q in range(G):
+            loads[n, q] = pltpu.make_async_copy(
+                src.at[:, cols[q]], dst.at[q], in_sem.at[n, q]
             )
-        ):
-            loads.append(pltpu.make_async_copy(src, dst, in_sem.at[n, q]))
-    for pick in ((0, 1), (2, 3)):
-        for q in range(G):
-            for n in pick:
-                loads[4 * q + n].start()
+    for q in range(KC):
+        part = pl.ds(KL * q, KL)
+        loads[2, q] = pltpu.make_async_copy(
+            hidden_hbm.at[:, part], hidden_scr.at[q], in_sem.at[2, q]
+        )
+        loads[3, q] = pltpu.make_async_copy(
+            w_hbm.at[part, :], w_scr.at[q], in_sem.at[3, q]
+        )
+    waves = [(loads[2, q], loads[3, q]) for q in range(KC)]
+    waves += [(loads[0, q], loads[1, q]) for q in range(G)]
+    ahead = 5
+
+    def take(n):
+        for load in waves[n]:
+            load.wait()
+        if n + ahead < len(waves):
+            for load in waves[n + ahead]:
+                load.start()
+
+    for wave in waves[:ahead]:
+        for load in wave:
+            load.start()
 
     eye = lax.broadcasted_iota(jnp.int32, (H, H), 0) == lax.broadcasted_iota(
         jnp.int32, (H, H), 1
     )
     rates = jnp.sum(jnp.where(eye, rates_ref[...], 0.0), axis=1, keepdims=True)
-    code = codes_ref[...].astype(F32)
+    s_at = lax.broadcasted_iota(jnp.int32, (T, T), 0)
+    t_at = lax.broadcasted_iota(jnp.int32, (T, T), 1)
+    upper = jnp.where(s_at <= t_at, 1.0, 0.0).astype(BF16)
+    onehot = spread_matrix()
+    cum_scr[...] = jnp.zeros_like(cum_scr)
+    code_load.wait()
+    code = codes_scr[...].astype(F32)
     step = -(
         rates * jnp.minimum(code, 1000.0) / 1000.0
         + 0.0005 * jnp.maximum(code - 1000.0, 0.0)
     )
-    s_at = lax.broadcasted_iota(jnp.int32, (T, T), 0)
-    t_at = lax.broadcasted_iota(jnp.int32, (T, T), 1)
-    upper = jnp.where(s_at <= t_at, 1.0, 0.0).astype(BF16)
     p1 = step.astype(BF16)
     rest = step - p1.astype(F32)
     p2 = rest.astype(BF16)
     p3 = (rest - p2.astype(F32)).astype(BF16)
     cum = mm(p1, upper) + mm(p2, upper) + mm(p3, upper)
-    group_scr[...] = jnp.zeros_like(group_scr)
-    onehot = spread_matrix()
+    stores = []
+
+    def send(src, dst, sem):
+        stores.append(pltpu.make_async_copy(src, dst, sem))
+        stores[-1].start()
+
     for q in range(G):
-        group_scr[q, 0:GH, :] = cum[GH * q : GH * (q + 1), :]
-        cum_ref[q] = group_scr[q, 0:16, :]
-        cumt_ref[q] = group_scr[q].T
-
-    acc = None
+        cum_scr[q, 0:GH, :] = cum[GH * q : GH * (q + 1), :]
+        full = jnp.concatenate([cum_scr[q], jnp.zeros((112, T), F32)])
+        cumt_scr[q] = full.T
+    send(cum_scr, cum_hbm, small_sem.at[1])
+    send(cumt_scr, cumt_hbm, small_sem.at[2])
+    for q in range(KC):
+        take(q)
+    depth = [hidden_scr[q] for q in range(KC)]
+    acc = mm(jnp.concatenate(depth, axis=1), w_scr[...].reshape(D, 2 * N))
+    bc_scr[...] = acc.astype(BF16)
+    send(bc_scr, bc_hbm, small_sem.at[3])
+    bt = bc_scr[:, :N].T
+    ct = bc_scr[:, N:].T
     for q in range(G):
-        loads[4 * q].wait()
-        loads[4 * q + 1].wait()
-        part = mm(hidden_scr[q], w_scr[q])
-        acc = part if acc is None else acc + part
-    bc_ref[...] = acc.astype(BF16)
-
-    stores = []
-    for q in range(G):
-        cumt = cumt_ref[q]
+        cumt = cumt_scr[q]
+        total = cumt[T - 1 : T, :]
         fw = spread(jnp.exp(cumt), onehot)
-        bw = spread(jnp.exp(cumt[T - 1 : T, :] - cumt), onehot)
-        loads[4 * q + 2].wait()
-        wi = (x_scr[q].astype(F32) * bw).astype(BF16)
-        loads[4 * q + 3].wait()
-        wg = (dy_scr[q].astype(F32) * fw).astype(BF16)
-        sf = mm_tn(bc_ref[:, :N], wi)
-        sb = mm_tn(bc_ref[:, N:], wg)
         decay = fw[T - 1 : T, :]
+        bw = spread(jnp.exp(total - cumt), onehot)
+        take(KC + q)
+        sf = mm(bt, (x_scr[q].astype(F32) * bw).astype(BF16))
+        sb = mm(ct, (dy_scr[q].astype(F32) * fw).astype(BF16))
+        rows = pl.ds(NM * q, NM)
         for n, (scr, hbm, state) in enumerate(
             (
                 (other_scr, other_hbm, jnp.where(is_first, sb, sf)),
@@ -148,22 +167,16 @@
                 scr[NM * q + m, STATE_ROWS + GT : ROWS, :] = jnp.zeros(
                     (ROWS - STATE_ROWS - GT, 128), F32
                 )
-            stores.append(
-                pltpu.make_async_copy(
-                    scr.at[slices[q]], hbm.at[slices[q]], out_sem.at[n, q]
-                )
-            )
-            stores[-1].start()
+            send(scr.at[rows], hbm.at[rows], out_sem.at[n, q])
     for store in stores:
         store.wait()
 
 
 def pre(core, hidden, w_bc, x, dy, codes, rates):
-    hbm = pl.BlockSpec(memory_space=pl.ANY)
     return pl.pallas_call(
         pre_kernel,
-        in_specs=[pl.BlockSpec(memory_space=pltpu.SMEM)] + [hbm] * 4 + [WHOLE] * 2,
-        out_specs=[WHOLE] * 3 + [hbm] * 2,
+        in_specs=[pl.BlockSpec(memory_space=pltpu.SMEM), WHOLE] + [IN_HBM] * 5,
+        out_specs=[IN_HBM] * 5,
         out_shape=[
             jax.ShapeDtypeStruct((T, 2 * N), BF16),
             jax.ShapeDtypeStruct((G, 16, T), F32),
@@ -172,25 +185,29 @@
             jax.ShapeDtypeStruct((CHIPS, ROWS, 128), F32),
         ],
         scratch_shapes=[
-            pltpu.VMEM((G, T, GL), BF16),
-            pltpu.VMEM((G, GL, 2 * N), BF16),
+            pltpu.VMEM((KC, T, KL), BF16),
+            pltpu.VMEM((KC, KL, 2 * N), BF16),
             pltpu.VMEM((G, T, GL), BF16),
             pltpu.VMEM((G, T, GL), BF16),
+            pltpu.VMEM((H, T), jnp.int32),
+            pltpu.VMEM((T, 2 * N), BF16),
+            pltpu.VMEM((G, 16, T), F32),
+            pltpu.VMEM((G, T, 128), F32),
             pltpu.VMEM((CHIPS, ROWS, 128), F32),
             pltpu.VMEM((CHIPS, ROWS, 128), F32),
-            pltpu.VMEM((G, 128, T), F32),
-            pltpu.SemaphoreType.DMA((4, G)),
+            pltpu.SemaphoreType.DMA((4, KC)),
             pltpu.SemaphoreType.DMA((2, G)),
+            pltpu.SemaphoreType.DMA((4,)),
         ],
         compiler_params=pltpu.CompilerParams(vmem_limit_bytes=LARGE),
         cost_estimate=pl.CostEstimate(
             flops=2 * 10**9, bytes_accessed=13 * 10**6, transcendentals=0
         ),
         name="pre",
-    )(core, hidden, w_bc, x, dy, codes, rates)
-
-
-def chip_kernel(mine_ref, got_ref, out_ref, token_ref):
+    )(core, rates, hidden, w_bc, x, dy, codes)
+
+
+def chip_kernel(mine_ref, got_ref, out_ref):
     for m in range(CHIPS):
         for i in range(GT):
             other = got_ref[m, STATE_ROWS + i : STATE_ROWS + i + 1, :]
@@ -198,21 +215,20 @@
             out_ref[m, rows, :] = other * mine_ref[m, rows, :] + got_ref[m, rows, :]
         tail = slice(STATE_ROWS, ROWS)
         out_ref[m, tail, :] = mine_ref[m, tail, :] * got_ref[m, tail, :]
-    token_ref[...] = jnp.zeros_like(token_ref)
 
 
 def chip_sum(mine, got):
     return pl.pallas_call(
         chip_kernel,
         in_specs=[WHOLE, WHOLE],
-        out_specs=[WHOLE, WHOLE],
-        out_shape=[jax.ShapeDtypeStruct((CHIPS, ROWS, 128), F32), token_shape()],
+        out_specs=WHOLE,
+        out_shape=jax.ShapeDtypeStruct((CHIPS, ROWS, 128), F32),
         compiler_params=pltpu.CompilerParams(vmem_limit_bytes=SMALL),
         name="chip_sum",
     )(mine, got)
 
 
-def scan_kernel(c_ref, in_ref, token_ref, out_ref):
+def scan_kernel(c_ref, in_ref, after_ref, out_ref):
     core = c_ref[0]
     state = [jnp.zeros((8, 128), F32) for _ in range(GT)]
     for k in range(CHIPS):
@@ -224,15 +240,15 @@
             state[i] = decay * state[i] + in_ref[at, rows, :]
 
 
-def scan_chips(core, slices, token):
+def scan_chips(core, slices, after):
     return pl.pallas_call(
         scan_kernel,
-        in_specs=[pl.BlockSpec(memory_space=pltpu.SMEM), WHOLE, WHOLE],
+        in_specs=[IN_SMEM, WHOLE, IN_SMEM],
         out_specs=WHOLE,
         out_shape=jax.ShapeDtypeStruct((CHIPS, STATE_ROWS, 128), F32),
         compiler_params=pltpu.CompilerParams(vmem_limit_bytes=SMALL),
         name="scan_chips",
-    )(core, slices, token)
+    )(core, slices, after)
 
 
 SPANS = ((0, 256), (0, 128), (256, 128))
@@ -301,7 +317,7 @@
         k = kmat[...].astype(BF16)
         dbc_ref[:, :N] = mm_tn(k, bc_ref[:, N:])
         dbc_ref[:, N:] = mm(k, bc_ref[:, :N])
-        token_ref[...] = jnp.zeros_like(token_ref)
+        token_ref[0] = 0
 
 
 def full_spec(*shape):
@@ -316,7 +332,7 @@
     return pl.BlockSpec((1, *shape), lambda q: (q, 0, 0))
 
 
-def pairs(core, bc, x, dy, cum, cumt, hidden, token):
+def pairs(core, bc, x, dy, cum, cumt, hidden, after):
     return pl.pallas_call(
         pairs_kernel,
         grid=(G,),
@@ -328,21 +344,21 @@
             group_spec(16, T),
             group_spec(T, 128),
             cols_spec(),
-            token_spec(),
+            IN_HBM,
         ],
         out_specs=[
             cols_spec(),
             cols_spec(),
             full_spec(T, 2 * N),
             pl.BlockSpec((GL, T), lambda q: (q, 0)),
-            token_spec(),
+            IN_SMEM,
         ],
         out_shape=[
             jax.ShapeDtypeStruct((T, D), BF16),
             jax.ShapeDtypeStruct((T, D), BF16),
             jax.ShapeDtypeStruct((T, 2 * N), F32),
             jax.ShapeDtypeStruct((D, T), BF16),
-            token_shape(),
+            TOKEN,
         ],
         scratch_shapes=[pltpu.VMEM((T, T), F32)],
         compiler_params=pltpu.CompilerParams(vmem_limit_bytes=LARGE),
@@ -350,7 +366,7 @@
             flops=20 * 10**9, bytes_accessed=16 * 10**6, transcendentals=3 * 10**6
         ),
         name="pairs",
-    )(core, bc, x, dy, cum, cumt, hidden, token)
+    )(core, bc, x, dy, cum, cumt, hidden, after)
 
 
 def carry_kernel(w_ref, came_ref, acc_ref, state_ref):
@@ -386,11 +402,20 @@
 
 
 def weight_kernel(
-    c_ref, accmine_ref, wother_ref, came_ref, theirs_ref, dbc_ref, turned_ref,
-    gwmine_ref, gwother_ref, state_ref,
+    c_ref, accmine_ref, wother_ref, came_ref, theirs_ref, dbc_ref, turned_hbm,
+    gwmine_ref, gwother_ref, state_ref, turned_scr, sem,
 ):
     core = c_ref[0]
     is_first = core == 0
+    starts = [pl.multiple_of(half * HALF_D, HALF_D) for half in (1 - core, core)]
+    loads = [
+        pltpu.make_async_copy(
+            turned_hbm.at[pl.ds(start, HALF_D), :], turned_scr.at[n], sem.at[n]
+        )
+        for n, start in enumerate(starts)
+    ]
+    for load in loads:
+        load.start()
     acc = jnp.zeros((T, N), F32)
     for q in range(G):
         for i in range(GT):
@@ -402,8 +427,8 @@
                 at = NM * q + m
                 pair = jnp.concatenate(
                     [
-                        decay * came_ref[a, rows, :] + theirs_ref[a, rows, :]
-                        for a in (at, at + 1)
+                        decay * came_ref[k, rows, :] + theirs_ref[k, rows, :]
+                        for k in (at, at + 1)
                     ]
                 )
                 state_ref[8 * m : 8 * m + 16, lanes] = pair.astype(BF16)
@@ -413,9 +438,9 @@
     db = dbc_ref[:, :N] + jnp.where(is_first, acc, mine)
     dc = dbc_ref[:, N:] + jnp.where(is_first, mine, acc)
     dbc = (jnp.concatenate([db, dc], axis=1) * (1.0 / (T * 2 * CHIPS))).astype(BF16)
-    for ref, half in ((gwother_ref, 1 - core), (gwmine_ref, core)):
-        start = pl.multiple_of(half * HALF_D, HALF_D)
-        part = mm(turned_ref[pl.ds(start, HALF_D), :], dbc)
+    for n, ref in enumerate((gwother_ref, gwmine_ref)):
+        loads[n].wait()
+        part = mm(turned_scr[n], dbc)
         ref[0] = part[:, :N]
         ref[1] = part[:, N:]
 
@@ -423,14 +448,18 @@
 def weight_part(core, acc_mine, w_other, came, theirs, dbc, turned):
     return pl.pallas_call(
         weight_kernel,
-        in_specs=[pl.BlockSpec(memory_space=pltpu.SMEM)] + [WHOLE] * 6,
+        in_specs=[IN_SMEM] + [WHOLE] * 5 + [IN_HBM],
         out_specs=[WHOLE, WHOLE, WHOLE],
         out_shape=[
             jax.ShapeDtypeStruct((2, HALF_D, N), F32),
             jax.ShapeDtypeStruct((2, HALF_D, N), F32),
             jax.ShapeDtypeStruct((N, D), BF16),
         ],
-        compiler_params=pltpu.CompilerParams(vmem_limit_bytes=20 << 20),
+        scratch_shapes=[
+            pltpu.VMEM((2, HALF_D, T), BF16),
+            pltpu.SemaphoreType.DMA((2,)),
+        ],
+        compiler_params=pltpu.CompilerParams(vmem_limit_bytes=MIDDLE),
         cost_estimate=pl.CostEstimate(
             flops=2 * 10**9, bytes_accessed=12 * 10**6, transcendentals=0
         ),
@@ -488,10 +517,10 @@
             gradx_ref[rows, lanes] = (
                 dxacc[rows, lanes] + jnp.where(first, dxs[0], dxs[1])
             ).astype(BF16)
-    token_ref[...] = jnp.zeros_like(token_ref)
-
-
-def outputs(core, bc, x, dy, cum, cumt, skip_row, s_mine, s_other, token):
+    token_ref[0] = 0
+
+
+def outputs(core, bc, x, dy, cum, cumt, skip_row, s_mine, s_other, after):
     return pl.pallas_call(
         outputs_kernel,
         grid=(G,),
@@ -505,13 +534,13 @@
             cols_spec(1),
             cols_spec(N),
             cols_spec(N),
-            token_spec(),
-        ],
-        out_specs=[cols_spec(), cols_spec(), token_spec()],
+            IN_HBM,
+        ],
+        out_specs=[cols_spec(), cols_spec(), IN_SMEM],
         out_shape=[
             jax.ShapeDtypeStruct((T, D), BF16),
             jax.ShapeDtypeStruct((T, D), BF16),
-            token_shape(),
+            TOKEN,
         ],
         scratch_shapes=[
             pltpu.VMEM((T, T), F32),
@@ -523,40 +552,56 @@
             flops=25 * 10**9, bytes_accessed=13 * 10**6, transcendentals=3 * 10**6
         ),
         name="outputs",
-    )(core, bc, x, dy, cum, cumt, skip_row, s_mine, s_other, token)
-
-
-def add_kernel(a_ref, b_ref, out_ref, token_ref):
-    out_ref[...] = a_ref[...] + b_ref[...]
-    token_ref[...] = jnp.zeros_like(token_ref)
+    )(core, bc, x, dy, cum, cumt, skip_row, s_mine, s_other, after)
+
+
+def add_kernel(a_ref, b_ref, out_hbm, scr, sem):
+    block = HALF_D // 2
+    stores = []
+    for lane in range(2):
+        for i in range(2):
+            rows = pl.ds(block * i, block)
+            scr[lane, rows, :] = a_ref[lane, rows, :] + b_ref[lane, rows, :]
+            stores.append(
+                pltpu.make_async_copy(
+                    scr.at[lane, rows], out_hbm.at[lane, rows], sem.at[lane, i]
+                )
+            )
+            stores[-1].start()
+    for store in stores:
+        store.wait()
 
 
 def pair_add(a, b):
     return pl.pallas_call(
         add_kernel,
         in_specs=[WHOLE, WHOLE],
-        out_specs=[WHOLE, WHOLE],
-        out_shape=[jax.ShapeDtypeStruct(a.shape, F32), token_shape()],
-        compiler_params=pltpu.CompilerParams(vmem_limit_bytes=SMALL),
+        out_specs=IN_HBM,
+        out_shape=jax.ShapeDtypeStruct(a.shape, F32),
+        scratch_shapes=[
+            pltpu.VMEM(a.shape, F32),
+            pltpu.SemaphoreType.DMA((2, 2)),
+        ],
+        compiler_params=pltpu.CompilerParams(vmem_limit_bytes=MIDDLE),
         name="pair_add",
     )(a, b)
 
 
-def total_kernel(in_ref, token_ref, out_ref):
+def total_kernel(in_ref, after_ref, out_ref):
     total = jnp.sum(in_ref[...], axis=0)
     for k in range(CHIPS):
         out_ref[k] = total
 
 
-def chip_total(parts, token):
+def chip_total(parts, after):
     return pl.pallas_call(
         total_kernel,
-        in_specs=[WHOLE, WHOLE],
+        in_specs=[WHOLE, IN_SMEM],
         out_specs=WHOLE,
         out_shape=jax.ShapeDtypeStruct((CHIPS, GW_ROWS, 128), F32),
         compiler_params=pltpu.CompilerParams(vmem_limit_bytes=SMALL),
         name="chip_total",
-    )(parts, token)
+    )(parts, after)
 
 
 def place_kernel(c_ref, half_ref, *refs):
@@ -598,23 +643,23 @@
     bc, cum, cumt, mine, other = pre(
         core, hidden, w_bc, ssm_in, grad_out, codes, rates[None, :]
     )
-    chip, token = chip_sum(mine, swap(other))
+    chip = chip_sum(mine, swap(other))
     slices = exchange(chip)
     theirs = swap(mine)
-    w_mine, w_other, dbc, turned, token = pairs(
-        core, bc, ssm_in, grad_out, cum, cumt, hidden, token
+    w_mine, w_other, dbc, turned, paired = pairs(
+        core, bc, ssm_in, grad_out, cum, cumt, hidden, chip
     )
-    came = exchange(scan_chips(core, slices, token))
+    came = exchange(scan_chips(core, slices, paired))
     acc_mine, s_mine = carry(w_mine, came)
     gw_mine, gw_other, s_other = weight_part(
         core, acc_mine, w_other, swap(came), theirs, dbc, turned
     )
-    part, token = pair_add(gw_mine, swap(gw_other))
+    part = pair_add(gw_mine, swap(gw_other))
     sums = exchange(part.reshape(CHIPS, GW_ROWS, 128))
-    mixed, gradx, token = outputs(
-        core, bc, ssm_in, grad_out, cum, cumt, skip_row, s_mine, s_other, token
+    mixed, gradx, done = outputs(
+        core, bc, ssm_in, grad_out, cum, cumt, skip_row, s_mine, s_other, part
     )
-    half = exchange(chip_total(sums, token)).reshape(2, HALF_D, 128)
+    half = exchange(chip_total(sums, done)).reshape(2, HALF_D, 128)
     grad_w = place(1 - core, swap(half), place(core, half, None))
     return mixed, gradx, grad_w
 

time: 157 us -> 155 us (0.987)
  local copies, waits for them, and re-layouts: 10.5 us -> 5.73 us
  Pallas kernels: 52.2 us -> 54.2 us
    unnamed x26 -> x14, local copies, waits for them, and re-layouts: 9.71 us -> 4.98 us
    pallas_call x5, Pallas kernels: 5.76 us -> 9.18 us  [the longest x1 4.1 us: weight_part(): pl.pallas_call(weight_kernel, in_specs=[IN_SMEM] + [WHOLE] * 5 + [IN_HBM]...]
where the time goes in v1:
time: 155 us; the launch traced here: 154 us
  Pallas kernels  54.2 us (35%)
  waiting for transfers between devices  34.4 us (22%)
  starting transfers between devices  31.8 us (21%)
  blocking collectives  27.2 us (18%)
  local copies, waits for them, and re-layouts  5.73 us (4%)
    all_to_all x3, waiting for transfers between devices, exchange(): return lax.all_to_all(v, CHIP_AXES, 0, 0, tiled=True)  27.2 us
    all_to_all x1, blocking collectives, exchange(): return lax.all_to_all(v, CHIP_AXES, 0, 0, tiled=True)  27.2 us
    all_to_all x3, starting transfers between devices, exchange(): return lax.all_to_all(v, CHIP_AXES, 0, 0, tiled=True)  21.5 us
    pallas_call x1, Pallas kernels, outputs(): pl.pallas_call(outputs_kernel, grid=(G,), in_specs=[pl.BlockSpec(memory_s...  18.3 us
    pallas_call x1, Pallas kernels, pairs(): pl.pallas_call(pairs_kernel, grid=(G,), in_specs=[pl.BlockSpec(memory_spa...  14 us
    ppermute x5, starting transfers between devices, swap(): return lax.ppermute(v, 'c', [(0, 1), (1, 0)])  10.3 us
    pallas_call x1, Pallas kernels, pre(): pl.pallas_call(pre_kernel, in_specs=[pl.BlockSpec(memory_space=pltpu.SMEM...  9.35 us
    ppermute x5, waiting for transfers between devices, swap(): return lax.ppermute(v, 'c', [(0, 1), (1, 0)])  7.19 us
  transfers between devices with their start and end apart: 8, of which 6 were waited for; matrix products, arithmetic and copies ran while one was open for 0% of the time, Pallas kernels for 22%

profile of v1, /device:TPU:1, one launch (start us, length us, event | category | flops | bytes accessed | tf_op | source)
XLA Modules:
  0.0 154.0 jit_solution(3480139448634798282)
XLA Ops:
  0.6 9.3 %pre.1 = (bf16[512,256]{1,0:T(8,128)(2,1)}, f32[4,16,512]{2,1,0:T(8,128)}, f32[4,512,128]{2,1,0:T(8,128)}, f32[64,48,128]{2,1,0:T(8,128)}, f32[64,48,128]{2,1,0:T(8,128)}) custom-call(s32[1]{0:T(128)} %bitcast.c_ref, f32[1,40]{1,0:T(1,128)} %bitcast.6, bf16[512,2560]{1,0:T(8,128)(2,1)} %hidden_ref.1, bf16[2560,256]{1,0:T(8,128)(2,1)} %w_hbm.1, ...), custom_call_target="tpu_custom_call" | custom-call | flops 2000000000 | bytes 13000000 | tf_op jit(solution)/shard_map/pre/pallas_call | solution.py:176
  10.0 1.5 collective-permute-start
  11.5 3.2 %collective-permute-done.got_ref = f32[64,48,128]{2,1,0:T(8,128)S(1)} collective-permute-done((f32[64,48,128]{2,1,0:T(8,128)}, f32[64,48,128]{2,1,0:T(8,128)S(1)}, u32[]{:S(2)}, u32[]{:S(2)}) %collective-permute-start) | collective-permute-done | bytes 1572896 | tf_op jit(solution)/shard_map/ppermute | solution.py:633
  14.7 0.0 copy-start.2
  14.7 1.4 copy-done.2
  16.1 1.4 chip_sum.1.after_ref
  17.5 11.2 %all-to-all-start = ((f32[64,48,128]{2,1,0:T(8,128)}), f32[64,48,128]{2,1,0:T(8,128)S(1)}, u32[]{:S(2)}, u32[]{:S(2)}) async-start(f32[64,48,128]{2,1,0:T(8,128)} %chip_sum.1.after_ref), calls=%async_computation | async-start | bytes 3145728 | tf_op jit(solution)/shard_map/all_to_all | solution.py:637
  28.7 14.0 %pairs.1 = (bf16[512,2560]{1,0:T(8,128)(2,1)}, bf16[512,2560]{1,0:T(8,128)(2,1)}, f32[512,256]{1,0:T(8,128)}, bf16[2560,512]{1,0:T(8,128)(2,1)}, s32[1]{0:T(128)}) custom-call(s32[1]{0:T(128)} %bitcast.c_ref, bf16[512,256]{1,0:T(8,128)(2,1)} %get-tuple-element.21.bc_ref, bf16[512,2560]{1,0:T(8,128)(2,1)} %x_ref.3, bf16[512,2560]{1,0:T(8,128)(2,1)} %dy_ref.3, ...), custom_call_target="tpu_custom_call" | custom-call | flops 20000000000 | bytes 16000000 | tf_op jit(solution)/shard_map/pairs/pallas_call | solution.py:336
  42.7 8.8 %all-to-all-done.in_ref = f32[64,48,128]{2,1,0:T(8,128)S(1)} async-done(((f32[64,48,128]{2,1,0:T(8,128)}), f32[64,48,128]{2,1,0:T(8,128)S(1)}, u32[]{:S(2)}, u32[]{:S(2)}) %all-to-all-start) | async-done | bytes 1572896 | tf_op jit(solution)/shard_map/all_to_all | solution.py:637
  51.5 1.9 %scan_chips.1 = f32[64,40,128]{2,1,0:T(8,128)} custom-call(s32[1]{0:T(128)} %bitcast.c_ref, f32[64,48,128]{2,1,0:T(8,128)S(1)} %all-to-all-done.in_ref, s32[1]{0:T(128)} %get-tuple-element.27.after_ref), custom_call_target="tpu_custom_call" | custom-call | tf_op jit(solution)/shard_map/scan_chips/pallas_call | solution.py:244
  53.4 5.5 %all-to-all-start.1 = ((f32[64,40,128]{2,1,0:T(8,128)}), f32[64,40,128]{2,1,0:T(8,128)S(1)}, u32[]{:S(2)}, u32[]{:S(2)}) async-start(f32[64,40,128]{2,1,0:T(8,128)} %scan_chips.1), calls=%async_computation.1 | async-start | bytes 2621440 | tf_op jit(solution)/shard_map/all_to_all | solution.py:637
  59.0 2.4 %collective-permute-start.2 = (f32[64,48,128]{2,1,0:T(8,128)}, f32[64,48,128]{2,1,0:T(8,128)S(1)}, u32[]{:S(2)}, u32[]{:S(2)}) collective-permute-start(f32[64,48,128]{2,1,0:T(8,128)} %get-tuple-element.24.mine_ref), channel_id=1, source_target_pairs={{0,1},{1,0},{2,3},{3,2},{4,5},{5,4},{6,7},{7,6},{8,9},{9,8},{10,11... | collective-permute-start | bytes 4718600 | tf_op jit(solution)/shard_map/ppermute | solution.py:633
  61.4 16.3 %all-to-all-done.1.came_ref = f32[64,40,128]{2,1,0:T(8,128)S(1)} async-done(((f32[64,40,128]{2,1,0:T(8,128)}), f32[64,40,128]{2,1,0:T(8,128)S(1)}, u32[]{:S(2)}, u32[]{:S(2)}) %all-to-all-start.1) | async-done | bytes 1310752 | tf_op jit(solution)/shard_map/all_to_all | solution.py:637
  77.7 3.7 %collective-permute-start.1 = (f32[64,40,128]{2,1,0:T(8,128)S(1)}, f32[64,40,128]{2,1,0:T(8,128)S(1)}, u32[]{:S(2)}, u32[]{:S(2)}) collective-permute-start(f32[64,40,128]{2,1,0:T(8,128)S(1)} %all-to-all-done.1.came_ref), channel_id=1, source_target_pairs={{0,1},{1,0},{2,3},{3,2},{4,5},{5,4},{6,7},{7,6},{8,9},{9,8},{10,11... | collective-permute-start | bytes 3932168 | tf_op jit(solution)/shard_map/ppermute | solution.py:633
  81.4 0.0 copy-start
  81.4 1.7 %copy-done = bf16[512,2560]{1,0:T(8,128)(2,1)S(1)} copy-done((bf16[512,2560]{1,0:T(8,128)(2,1)S(1)}, bf16[512,2560]{1,0:T(8,128)(2,1)}, u32[]{:S(2)}) %copy-start) | copy-done | bytes 2621464
  83.1 0.0 copy-start.1
  83.1 0.0 copy-start.3
  83.1 0.9 carry.1
  84.0 0.0 copy-start.4
  84.0 0.8 copy-done.4
  84.8 0.0 collective-permute-done.2.theirs_ref
  84.8 0.0 collective-permute-done.1.came_ref
  84.8 0.0 copy-done.1
  84.8 0.2 copy-done.3
  85.0 0.0 copy-start.6
  85.0 4.1 %weight_part.1 = (f32[2,1280,128]{2,1,0:T(8,128)S(1)}, f32[2,1280,128]{2,1,0:T(8,128)}, bf16[128,2560]{1,0:T(8,128)(2,1)S(1)}) custom-call(s32[1]{0:T(128)} %bitcast.c_ref, f32[512,128]{1,0:T(8,128)S(1)} %get-tuple-element.29.accmine_ref, bf16[512,2560]{1,0:T(8,128)(2,1)S(1)} %copy-done.1, f32[64,40,128]{2,1,0:T(8,128)S(1)} %collective-permute-done.1.came_ref, ...), custom_call_target="tpu_custom_call" | custom-call | flops 2000000000 | bytes 12000000 | tf_op jit(solution)/shard_map/weight_part/pallas_call | solution.py:449
  89.1 0.0 copy-start.5
  89.1 0.8 copy-done.5
  90.0 0.0 collective-permute-start.3
  90.0 0.0 copy-done.6
  90.0 0.1 broadcast_in_dim.7
  90.0 0.7 broadcast_in_dim_reshape.3.skip_ref
  90.7 2.5 %collective-permute-done.3.b_ref = f32[2,1280,128]{2,1,0:T(8,128)S(1)} collective-permute-done((f32[2,1280,128]{2,1,0:T(8,128)}, f32[2,1280,128]{2,1,0:T(8,128)S(1)}, u32[]{:S(2)}, u32[]{:S(2)}) %collective-permute-start.3) | collective-permute-done | bytes 1310752 | tf_op jit(solution)/shard_map/ppermute | solution.py:633
  93.2 1.1 pair_add.1.after_ref
  94.3 4.7 %all-to-all-start.2 = ((f32[64,40,128]{2,1,0:T(8,128)}), f32[64,40,128]{2,1,0:T(8,128)S(1)}, u32[]{:S(2)}, u32[]{:S(2)}) async-start(f32[64,40,128]{2,1,0:T(8,128)} %bitcast.2), calls=%async_computation.2 | async-start | bytes 2621440 | tf_op jit(solution)/shard_map/all_to_all | solution.py:637
  99.1 18.3 %outputs.1 = (bf16[512,2560]{1,0:T(8,128)(2,1)}, bf16[512,2560]{1,0:T(8,128)(2,1)}, s32[1]{0:T(128)}) custom-call(s32[1]{0:T(128)} %bitcast.c_ref, bf16[512,256]{1,0:T(8,128)(2,1)} %get-tuple-element.21.bc_ref, bf16[512,2560]{1,0:T(8,128)(2,1)} %x_ref.3, bf16[512,2560]{1,0:T(8,128)(2,1)} %dy_ref.3, f32[4,16,512]{2,1,0:T(8,128)} %get-tuple-element.22.cum_ref, ...), custom_call_target="tpu_custom_call" | custom-call | flops 24999999488 | bytes 13000000 | tf_op jit(solution)/shard_map/outputs/pallas_call | solution.py:524
  117.4 2.2 %all-to-all-done.2.in_ref = f32[64,40,128]{2,1,0:T(8,128)S(1)} async-done(((f32[64,40,128]{2,1,0:T(8,128)}), f32[64,40,128]{2,1,0:T(8,128)S(1)}, u32[]{:S(2)}, u32[]{:S(2)}) %all-to-all-start.2) | async-done | bytes 1310752 | tf_op jit(solution)/shard_map/all_to_all | solution.py:637
  119.6 0.7 chip_total.1
  120.3 27.2 %all_to_all.20 = f32[64,40,128]{2,1,0:T(8,128)S(1)} all-to-all(f32[64,40,128]{2,1,0:T(8,128)S(1)} %chip_total.1), channel_id=1, replica_groups=mesh['z'=4,'x'=4,'y'=4,'c'=2] {'z','x','y'}, dimensions={0} | all-to-all | bytes 2621440 | tf_op jit(solution)/shard_map/all_to_all | solution.py:637
  147.5 2.6 %collective-permute-start.4 = (f32[2,1280,128]{2,1,0:T(8,128)S(1)}, f32[2,1280,128]{2,1,0:T(8,128)S(1)}, u32[]{:S(2)}, u32[]{:S(2)}) collective-permute-start(f32[2,1280,128]{2,1,0:T(8,128)S(1)} %bitcast.4), channel_id=1, source_target_pairs={{0,1},{1,0},{2,3},{3,2},{4,5},{5,4},{6,7},{7,6},{8,9},{9,8},{10,11... | collective-permute-start | bytes 3932168 | tf_op jit(solution)/shard_map/ppermute | solution.py:633
  150.1 1.2 place.2.refs_0_
  151.3 1.5 collective-permute-done.4.half_ref
  152.8 1.2 place.3
Async XLA Ops:
  10.0 4.7 %collective-permute-start = (f32[64,48,128]{2,1,0:T(8,128)}, f32[64,48,128]{2,1,0:T(8,128)S(1)}, u32[]{:S(2)}, u32[]{:S(2)}) collective-permute-start(f32[64,48,128]{2,1,0:T(8,128)} %get-tuple-element.25), channel_id=1, source_target_pairs={{0,1},{1,0},{2,3},{3,2},{4,5},{5,4},{6,7},{7,6},{8,9},{9,8},{10,11... | collective-permute-start | bytes 4718600 | tf_op jit(solution)/shard_map/ppermute | solution.py:633
  14.7 1.4 copy-start.2
  17.5 34.0 %all-to-all-start = ((f32[64,48,128]{2,1,0:T(8,128)}), f32[64,48,128]{2,1,0:T(8,128)S(1)}, u32[]{:S(2)}, u32[]{:S(2)}) async-start(f32[64,48,128]{2,1,0:T(8,128)} %chip_sum.1.after_ref), calls=%async_computation | async-start | bytes 3145728 | tf_op jit(solution)/shard_map/all_to_all | solution.py:637
  53.4 24.3 %all-to-all-start.1 = ((f32[64,40,128]{2,1,0:T(8,128)}), f32[64,40,128]{2,1,0:T(8,128)S(1)}, u32[]{:S(2)}, u32[]{:S(2)}) async-start(f32[64,40,128]{2,1,0:T(8,128)} %scan_chips.1), calls=%async_computation.1 | async-start | bytes 2621440 | tf_op jit(solution)/shard_map/all_to_all | solution.py:637
  59.0 25.9 %collective-permute-start.2 = (f32[64,48,128]{2,1,0:T(8,128)}, f32[64,48,128]{2,1,0:T(8,128)S(1)}, u32[]{:S(2)}, u32[]{:S(2)}) collective-permute-start(f32[64,48,128]{2,1,0:T(8,128)} %get-tuple-element.24.mine_ref), channel_id=1, source_target_pairs={{0,1},{1,0},{2,3},{3,2},{4,5},{5,4},{6,7},{7,6},{8,9},{9,8},{10,11... | collective-permute-start | bytes 4718600 | tf_op jit(solution)/shard_map/ppermute | solution.py:633
  77.7 7.2 %collective-permute-start.1 = (f32[64,40,128]{2,1,0:T(8,128)S(1)}, f32[64,40,128]{2,1,0:T(8,128)S(1)}, u32[]{:S(2)}, u32[]{:S(2)}) collective-permute-start(f32[64,40,128]{2,1,0:T(8,128)S(1)} %all-to-all-done.1.came_ref), channel_id=1, source_target_pairs={{0,1},{1,0},{2,3},{3,2},{4,5},{5,4},{6,7},{7,6},{8,9},{9,8},{10,11... | collective-permute-start | bytes 3932168 | tf_op jit(solution)/shard_map/ppermute | solution.py:633
  81.4 1.7 %copy-start = (bf16[512,2560]{1,0:T(8,128)(2,1)S(1)}, bf16[512,2560]{1,0:T(8,128)(2,1)}, u32[]{:S(2)}) copy-start(bf16[512,2560]{1,0:T(8,128)(2,1)} %get-tuple-element.26.w_ref) | copy-start | bytes 7864324
  83.1 1.7 %copy-start.1 = (bf16[512,2560]{1,0:T(8,128)(2,1)S(1)}, bf16[512,2560]{1,0:T(8,128)(2,1)}, u32[]{:S(2)}) copy-start(bf16[512,2560]{1,0:T(8,128)(2,1)} %get-tuple-element.30.wother_ref) | copy-start | bytes 7864324
  83.1 1.9 %copy-start.3 = (f32[512,256]{1,0:T(8,128)S(1)}, f32[512,256]{1,0:T(8,128)}, u32[]{:S(2)}) copy-start(f32[512,256]{1,0:T(8,128)} %get-tuple-element.31.dbc_ref) | copy-start | bytes 1572868
  84.0 0.8 copy-start.4
  85.0 5.0 %copy-start.6 = (f32[40]{0:T(128)S(1)}, f32[40]{0:T(128)}, u32[]{:S(2)}) copy-start(f32[40]{0:T(128)} %param.12) | copy-start | bytes 484
  89.1 0.9 copy-start.5
  90.0 3.2 %collective-permute-start.3 = (f32[2,1280,128]{2,1,0:T(8,128)}, f32[2,1280,128]{2,1,0:T(8,128)S(1)}, u32[]{:S(2)}, u32[]{:S(2)}) collective-permute-start(f32[2,1280,128]{2,1,0:T(8,128)} %get-tuple-element.35), channel_id=1, source_target_pairs={{0,1},{1,0},{2,3},{3,2},{4,5},{5,4},{6,7},{7,6},{8,9},{9,8},{10,11... | collective-permute-start | bytes 3932168 | tf_op jit(solution)/shard_map/ppermute | solution.py:633
  94.3 25.2 %all-to-all-start.2 = ((f32[64,40,128]{2,1,0:T(8,128)}), f32[64,40,128]{2,1,0:T(8,128)S(1)}, u32[]{:S(2)}, u32[]{:S(2)}) async-start(f32[64,40,128]{2,1,0:T(8,128)} %bitcast.2), calls=%async_computation.2 | async-start | bytes 2621440 | tf_op jit(solution)/shard_map/all_to_all | solution.py:637
  147.5 5.3 %collective-permute-start.4 = (f32[2,1280,128]{2,1,0:T(8,128)S(1)}, f32[2,1280,128]{2,1,0:T(8,128)S(1)}, u32[]{:S(2)}, u32[]{:S(2)}) collective-permute-start(f32[2,1280,128]{2,1,0:T(8,128)S(1)} %bitcast.4), channel_id=1, source_target_pairs={{0,1},{1,0},{2,3},{3,2},{4,5},{5,4},{6,7},{7,6},{8,9},{9,8},{10,11... | collective-permute-start | bytes 3932168 | tf_op jit(solution)/shard_map/ppermute | solution.py:633

commit v2 on v1

--- a/solution.py
+++ b/solution.py
@@ -26,7 +26,8 @@
 STATE_ROWS = 8 * GT
 ROWS = 48
 HALF_D = D // 2
-GW_ROWS = 40
+PLANE = 16
+GW_ROWS = 2 * HALF_D // PLANE
 KC = 5
 KL = D // KC
 LARGE = 56 << 20
@@ -468,9 +469,9 @@
 
 
 def outputs_kernel(
-    c_ref, bc_ref, x_ref, dy_ref, cum_ref, cumt_ref, skip_ref, smine_ref, sother_ref, after_ref,
-    mixed_ref, gradx_ref, token_ref, scores, yacc, dxacc,
+    c_ref, bc_ref, x_ref, dy_ref, cum_ref, cumt_ref, skip_ref, smine_ref, sother_ref, *refs,
 ):
+    mixed_ref, gradx_ref, token_ref, scores, yacc, dxacc = refs[-6:]
     is_first = c_ref[0] == 0
     b_mat = bc_ref[:, :N]
     c_mat = bc_ref[:, N:]
@@ -517,26 +518,28 @@
             gradx_ref[rows, lanes] = (
                 dxacc[rows, lanes] + jnp.where(first, dxs[0], dxs[1])
             ).astype(BF16)
-    token_ref[0] = 0
-
-
-def outputs(core, bc, x, dy, cum, cumt, skip_row, s_mine, s_other, after):
+    token_ref[0] = c_ref[0]
+
+
+def outputs(core, bc, x, dy, cum, cumt, skip_row, s_mine, s_other, start, extra):
+    cols = lambda rows=T: pl.BlockSpec((rows, GL), lambda q: (0, q + start))
+    group = lambda *shape: pl.BlockSpec((1, *shape), lambda q: (q + start, 0, 0))
     return pl.pallas_call(
         outputs_kernel,
-        grid=(G,),
+        grid=(G // 2,),
         in_specs=[
-            pl.BlockSpec(memory_space=pltpu.SMEM),
+            IN_SMEM,
             full_spec(T, 2 * N),
-            cols_spec(),
-            cols_spec(),
-            group_spec(16, T),
-            group_spec(T, 128),
-            cols_spec(1),
-            cols_spec(N),
-            cols_spec(N),
-            IN_HBM,
-        ],
-        out_specs=[cols_spec(), cols_spec(), IN_SMEM],
+            cols(),
+            cols(),
+            group(16, T),
+            group(T, 128),
+            cols(1),
+            cols(N),
+            cols(N),
+        ]
+        + [IN_HBM] * len(extra),
+        out_specs=[cols(), cols(), IN_SMEM],
         out_shape=[
             jax.ShapeDtypeStruct((T, D), BF16),
             jax.ShapeDtypeStruct((T, D), BF16),
@@ -547,12 +550,13 @@
             pltpu.VMEM((T, GL), F32),
             pltpu.VMEM((T, GL), F32),
         ],
+        input_output_aliases={9: 0, 10: 1} if len(extra) == 2 else {},
         compiler_params=pltpu.CompilerParams(vmem_limit_bytes=LARGE),
         cost_estimate=pl.CostEstimate(
-            flops=25 * 10**9, bytes_accessed=13 * 10**6, transcendentals=3 * 10**6
+            flops=12 * 10**9, bytes_accessed=7 * 10**6, transcendentals=2 * 10**6
         ),
         name="outputs",
-    )(core, bc, x, dy, cum, cumt, skip_row, s_mine, s_other, after)
+    )(core, bc, x, dy, cum, cumt, skip_row, s_mine, s_other, *extra)
 
 
 def add_kernel(a_ref, b_ref, out_hbm, scr, sem):
@@ -587,21 +591,64 @@
     )(a, b)
 
 
-def total_kernel(in_ref, after_ref, out_ref):
-    total = jnp.sum(in_ref[...], axis=0)
-    for k in range(CHIPS):
-        out_ref[k] = total
-
-
-def chip_total(parts, after):
-    return pl.pallas_call(
-        total_kernel,
+def plane_kernel(in_ref, after_ref, out_ref):
+    out_ref[...] = jnp.sum(in_ref[...], axis=0)
+
+
+def plane_total(parts, after):
+    return pl.pallas_call(
+        plane_kernel,
         in_specs=[WHOLE, IN_SMEM],
         out_specs=WHOLE,
-        out_shape=jax.ShapeDtypeStruct((CHIPS, GW_ROWS, 128), F32),
+        out_shape=jax.ShapeDtypeStruct((GW_ROWS, 128), F32),
         compiler_params=pltpu.CompilerParams(vmem_limit_bytes=SMALL),
-        name="chip_total",
+        name="plane_total",
     )(parts, after)
+
+
+def chips_kernel(c_ref, z_ref, own_ref, back1_ref, back2_ref, back3_ref, out_ref, token_ref):
+    z = z_ref[0]
+    held = [own_ref[...], back1_ref[...], back2_ref[...], back3_ref[...]]
+    total = None
+    for plane in range(4):
+        behind = jnp.bitwise_and(z - plane, 3)
+        part = held[3]
+        for k in range(3):
+            part = jnp.where(behind == k, held[k], part)
+        total = part if total is None else total + part
+    for k in range(PLANE):
+        out_ref[k] = total
+    token_ref[0] = c_ref[0]
+
+
+def chips_total(core, z, own):
+    others = [
+        lax.ppermute(own, "z", [(i, (i + k) % 4) for i in range(4)]) for k in (1, 2, 3)
+    ]
+    return pl.pallas_call(
+        chips_kernel,
+        in_specs=[IN_SMEM] * 2 + [WHOLE] * 4,
+        out_specs=[WHOLE, IN_SMEM],
+        out_shape=[jax.ShapeDtypeStruct((PLANE, GW_ROWS, 128), F32), TOKEN],
+        compiler_params=pltpu.CompilerParams(vmem_limit_bytes=SMALL),
+        name="chips_total",
+    )(core, z, own, *others)
+
+
+def hold_kernel(c_ref, in_ref, out_ref, token_ref):
+    out_ref[...] = in_ref[...]
+    token_ref[0] = c_ref[0]
+
+
+def hold(core, half):
+    return pl.pallas_call(
+        hold_kernel,
+        in_specs=[IN_SMEM, WHOLE],
+        out_specs=[WHOLE, IN_SMEM],
+        out_shape=[jax.ShapeDtypeStruct(half.shape, F32), TOKEN],
+        compiler_params=pltpu.CompilerParams(vmem_limit_bytes=SMALL),
+        name="hold",
+    )(core, half)
 
 
 def place_kernel(c_ref, half_ref, *refs):
@@ -633,8 +680,8 @@
     return lax.ppermute(v, "c", [(0, 1), (1, 0)])
 
 
-def exchange(v):
-    return lax.all_to_all(v, CHIP_AXES, 0, 0, tiled=True)
+def exchange(v, axes=CHIP_AXES):
+    return lax.all_to_all(v, axes, 0, 0, tiled=True)
 
 
 def shards(hidden, w_bc, ssm_in, codes, rates, skip, grad_out):
@@ -655,12 +702,15 @@
         core, acc_mine, w_other, swap(came), theirs, dbc, turned
     )
     part = pair_add(gw_mine, swap(gw_other))
-    sums = exchange(part.reshape(CHIPS, GW_ROWS, 128))
-    mixed, gradx, done = outputs(
-        core, bc, ssm_in, grad_out, cum, cumt, skip_row, s_mine, s_other, part
-    )
-    half = exchange(chip_total(sums, done)).reshape(2, HALF_D, 128)
-    grad_w = place(1 - core, swap(half), place(core, half, None))
+    sums = exchange(part.reshape(PLANE, GW_ROWS, 128), ("x", "y"))
+    pieces = (bc, ssm_in, grad_out, cum, cumt, skip_row, s_mine, s_other)
+    mixed, gradx, done = outputs(core, *pieces, 0, [part])
+    z = lax.axis_index("z").astype(jnp.int32).reshape(1)
+    total, core_after = chips_total(core, z, plane_total(sums, done))
+    half = exchange(total, ("x", "y")).reshape(2, HALF_D, 128)
+    mixed, gradx, core_after = outputs(core_after, *pieces, G // 2, [mixed, gradx])
+    half, core_after = hold(core_after, half)
+    grad_w = place(1 - core, swap(half), place(core_after, half, None))
     return mixed, gradx, grad_w
 
 

time: 155 us -> 157 us (1.013)
  blocking collectives: 27.2 us -> 0 us
  waiting for transfers between devices: 34.4 us -> 50.8 us
  starting transfers between devices: 31.8 us -> 38.6 us
  Pallas kernels: 54.2 us -> 60.9 us
    all_to_all x1 -> x0, blocking collectives: 27.2 us -> none  [exchange(): return lax.all_to_all(v, CHIP_AXES, 0, 0, tiled=True)]
    all_to_all x3 -> x4, waiting for transfers between devices: 27.2 us -> 40.2 us  [exchange(): return lax.all_to_all(v, axes, 0, 0, tiled=True)]
    pallas_call x2 -> x5, Pallas kernels: 19.1 us -> 25.3 us  [the longest x2 22.2 us: outputs(): pl.pallas_call(outputs_kernel, grid=(G // 2,), in_specs=[IN_SMEM, full_sp...]
    ppermute x0 -> x3, waiting for transfers between devices: none -> 3.57 us  [chips_total(): lax.ppermute(own, 'z', [(i, (i + k) % 4) for i in range(4)])]
    all_to_all x3 -> x4, starting transfers between devices: 21.5 us -> 24.4 us  [exchange(): return lax.all_to_all(v, axes, 0, 0, tiled=True)]
    ppermute x0 -> x3, starting transfers between devices: none -> 2.74 us  [chips_total(): lax.ppermute(own, 'z', [(i, (i + k) % 4) for i in range(4)])]
  transfers between devices with their start and end apart: 8 -> 12, of which waited for: 6 -> 10; matrix products, arithmetic and copies ran while one was open for 0% -> 0% of each run, Pallas kernels for 22% -> 25%
where the time goes in v2:
time: 157 us; the launch traced here: 156 us
  Pallas kernels  60.9 us (39%)
  waiting for transfers between devices  50.8 us (32%)
  starting transfers between devices  38.6 us (25%)
  local copies, waits for them, and re-layouts  4.89 us (3%)
    all_to_all x4, waiting for transfers between devices, exchange(): return lax.all_to_all(v, axes, 0, 0, tiled=True)  40.2 us
    all_to_all x4, starting transfers between devices, exchange(): return lax.all_to_all(v, axes, 0, 0, tiled=True)  24.4 us
    pallas_call x2, Pallas kernels, outputs(): pl.pallas_call(outputs_kernel, grid=(G // 2,), in_specs=[IN_SMEM, full_sp...  22.2 us
    pallas_call x1, Pallas kernels, pairs(): pl.pallas_call(pairs_kernel, grid=(G,), in_specs=[pl.BlockSpec(memory_spa...  14 us
    ppermute x5, starting transfers between devices, swap(): return lax.ppermute(v, 'c', [(0, 1), (1, 0)])  11.5 us
    pallas_call x1, Pallas kernels, pre(): pl.pallas_call(pre_kernel, in_specs=[pl.BlockSpec(memory_space=pltpu.SMEM...  9.37 us
    ppermute x5, waiting for transfers between devices, swap(): return lax.ppermute(v, 'c', [(0, 1), (1, 0)])  7.02 us
    unnamed x14, local copies, waits for them, and re-layouts  4.13 us
  transfers between devices with their start and end apart: 12, of which 10 were waited for; matrix products, arithmetic and copies ran while one was open for 0% of the time, Pallas kernels for 25%

profile of v2, /device:TPU:1, one launch (start us, length us, event | category | flops | bytes accessed | tf_op | source)
XLA Modules:
  0.0 156.0 jit_solution(5831432964881658556)
XLA Ops:
  0.6 9.4 %pre.1 = (bf16[512,256]{1,0:T(8,128)(2,1)}, f32[4,16,512]{2,1,0:T(8,128)}, f32[4,512,128]{2,1,0:T(8,128)}, f32[64,48,128]{2,1,0:T(8,128)}, f32[64,48,128]{2,1,0:T(8,128)}) custom-call(s32[1]{0:T(128)} %bitcast.c_ref, f32[1,40]{1,0:T(1,128)} %bitcast.6, bf16[512,2560]{1,0:T(8,128)(2,1)} %hidden_ref.1, bf16[2560,256]{1,0:T(8,128)(2,1)} %w_hbm.1, ...), custom_call_target="tpu_custom_call" | custom-call | flops 2000000000 | bytes 13000000 | tf_op jit(solution)/shard_map/pre/pallas_call | solution.py:177
  10.0 1.5 collective-permute-start
  11.5 3.2 %collective-permute-done.got_ref = f32[64,48,128]{2,1,0:T(8,128)S(1)} collective-permute-done((f32[64,48,128]{2,1,0:T(8,128)}, f32[64,48,128]{2,1,0:T(8,128)S(1)}, u32[]{:S(2)}, u32[]{:S(2)}) %collective-permute-start) | collective-permute-done | bytes 1572896 | tf_op jit(solution)/shard_map/ppermute | solution.py:680
  14.8 0.0 copy-start.2
  14.8 1.4 copy-done.2
  16.2 1.4 chip_sum.1.after_ref
  17.5 11.2 %all-to-all-start = ((f32[64,48,128]{2,1,0:T(8,128)}), f32[64,48,128]{2,1,0:T(8,128)S(1)}, u32[]{:S(2)}, u32[]{:S(2)}) async-start(f32[64,48,128]{2,1,0:T(8,128)} %chip_sum.1.after_ref), calls=%async_computation | async-start | bytes 3145728 | tf_op jit(solution)/shard_map/all_to_all | solution.py:684
  28.7 14.0 %pairs.1 = (bf16[512,2560]{1,0:T(8,128)(2,1)}, bf16[512,2560]{1,0:T(8,128)(2,1)}, f32[512,256]{1,0:T(8,128)}, bf16[2560,512]{1,0:T(8,128)(2,1)}, s32[1]{0:T(128)}) custom-call(s32[1]{0:T(128)} %bitcast.c_ref, bf16[512,256]{1,0:T(8,128)(2,1)} %get-tuple-element.28.bc_ref, bf16[512,2560]{1,0:T(8,128)(2,1)} %x_ref.5, bf16[512,2560]{1,0:T(8,128)(2,1)} %dy_ref.5, ...), custom_call_target="tpu_custom_call" | custom-call | flops 20000000000 | bytes 16000000 | tf_op jit(solution)/shard_map/pairs/pallas_call | solution.py:337
  42.7 8.8 %all-to-all-done.in_ref = f32[64,48,128]{2,1,0:T(8,128)S(1)} async-done(((f32[64,48,128]{2,1,0:T(8,128)}), f32[64,48,128]{2,1,0:T(8,128)S(1)}, u32[]{:S(2)}, u32[]{:S(2)}) %all-to-all-start) | async-done | bytes 1572896 | tf_op jit(solution)/shard_map/all_to_all | solution.py:684
  51.5 2.0 %scan_chips.1 = f32[64,40,128]{2,1,0:T(8,128)} custom-call(s32[1]{0:T(128)} %bitcast.c_ref, f32[64,48,128]{2,1,0:T(8,128)S(1)} %all-to-all-done.in_ref, s32[1]{0:T(128)} %get-tuple-element.34.after_ref), custom_call_target="tpu_custom_call" | custom-call | tf_op jit(solution)/shard_map/scan_chips/pallas_call | solution.py:245
  53.6 5.5 %all-to-all-start.1 = ((f32[64,40,128]{2,1,0:T(8,128)}), f32[64,40,128]{2,1,0:T(8,128)S(1)}, u32[]{:S(2)}, u32[]{:S(2)}) async-start(f32[64,40,128]{2,1,0:T(8,128)} %scan_chips.1), calls=%async_computation.1 | async-start | bytes 2621440 | tf_op jit(solution)/shard_map/all_to_all | solution.py:684
  59.1 2.4 %collective-permute-start.2 = (f32[64,48,128]{2,1,0:T(8,128)}, f32[64,48,128]{2,1,0:T(8,128)S(1)}, u32[]{:S(2)}, u32[]{:S(2)}) collective-permute-start(f32[64,48,128]{2,1,0:T(8,128)} %get-tuple-element.31.mine_ref), channel_id=1, source_target_pairs={{0,1},{1,0},{2,3},{3,2},{4,5},{5,4},{6,7},{7,6},{8,9},{9,8},{10,11... | collective-permute-start | bytes 4718600 | tf_op jit(solution)/shard_map/ppermute | solution.py:680
  61.5 16.3 %all-to-all-done.1.came_ref = f32[64,40,128]{2,1,0:T(8,128)S(1)} async-done(((f32[64,40,128]{2,1,0:T(8,128)}), f32[64,40,128]{2,1,0:T(8,128)S(1)}, u32[]{:S(2)}, u32[]{:S(2)}) %all-to-all-start.1) | async-done | bytes 1310752 | tf_op jit(solution)/shard_map/all_to_all | solution.py:684
  77.8 3.7 %collective-permute-start.1 = (f32[64,40,128]{2,1,0:T(8,128)S(1)}, f32[64,40,128]{2,1,0:T(8,128)S(1)}, u32[]{:S(2)}, u32[]{:S(2)}) collective-permute-start(f32[64,40,128]{2,1,0:T(8,128)S(1)} %all-to-all-done.1.came_ref), channel_id=1, source_target_pairs={{0,1},{1,0},{2,3},{3,2},{4,5},{5,4},{6,7},{7,6},{8,9},{9,8},{10,11... | collective-permute-start | bytes 3932168 | tf_op jit(solution)/shard_map/ppermute | solution.py:680
  81.5 0.0 copy-start
  81.5 1.7 %copy-done = bf16[512,2560]{1,0:T(8,128)(2,1)S(1)} copy-done((bf16[512,2560]{1,0:T(8,128)(2,1)S(1)}, bf16[512,2560]{1,0:T(8,128)(2,1)}, u32[]{:S(2)}) %copy-start) | copy-done | bytes 2621464
  83.2 0.0 copy-start.1
  83.2 0.0 copy-start.3
  83.2 0.9 carry.1
  84.1 0.0 copy-start.4
  84.2 0.0 collective-permute-done.2.theirs_ref
  84.2 0.0 collective-permute-done.1.came_ref
  84.2 0.8 copy-done.1
  85.0 0.2 copy-done.3
  85.1 3.7 %weight_part.1 = (f32[2,1280,128]{2,1,0:T(8,128)S(1)}, f32[2,1280,128]{2,1,0:T(8,128)S(1)}, bf16[128,2560]{1,0:T(8,128)(2,1)S(1)}) custom-call(s32[1]{0:T(128)} %bitcast.c_ref, f32[512,128]{1,0:T(8,128)S(1)} %get-tuple-element.35.accmine_ref, bf16[512,2560]{1,0:T(8,128)(2,1)S(1)} %copy-done.1, f32[64,40,128]{2,1,0:T(8,128)S(1)} %collective-permute-done.1.came_ref, ...), custom_call_target="tpu_custom_call" | custom-call | flops 2000000000 | bytes 12000000 | tf_op jit(solution)/shard_map/weight_part/pallas_call | solution.py:450
  88.8 0.0 copy-done.4
  88.8 0.0 copy-start.5
  88.9 0.1 collective-permute-start.3
  88.9 3.0 %collective-permute-done.3.b_ref = f32[2,1280,128]{2,1,0:T(8,128)S(1)} collective-permute-done((f32[2,1280,128]{2,1,0:T(8,128)S(1)}, f32[2,1280,128]{2,1,0:T(8,128)S(1)}, u32[]{:S(2)}, u32[]{:S(2)}) %collective-permute-start.3) | collective-permute-done | bytes 1310752 | tf_op jit(solution)/shard_map/ppermute | solution.py:680
  92.0 1.1 pair_add.1.refs_0_
  93.1 0.0 copy-done.5
  93.1 0.0 copy-start.6
  93.1 3.7 %all-to-all-start.2 = ((f32[16,160,128]{2,1,0:T(8,128)}), f32[16,160,128]{2,1,0:T(8,128)S(1)}, u32[]{:S(2)}, u32[]{:S(2)}) async-start(f32[16,160,128]{2,1,0:T(8,128)} %bitcast.3), calls=%async_computation.2 | async-start | bytes 2621440 | tf_op jit(solution)/shard_map/all_to_all | solution.py:684
  96.8 0.0 copy-done.6
  96.8 0.1 broadcast_in_dim.7
  96.9 0.7 broadcast_in_dim_reshape.3.skip_ref
  97.6 10.8 %outputs.2 = (bf16[512,2560]{1,0:T(8,128)(2,1)}, bf16[512,2560]{1,0:T(8,128)(2,1)}, s32[1]{0:T(128)}) custom-call(s32[1]{0:T(128)} %bitcast.c_ref, bf16[512,256]{1,0:T(8,128)(2,1)} %get-tuple-element.28.bc_ref, bf16[512,2560]{1,0:T(8,128)(2,1)} %x_ref.5, bf16[512,2560]{1,0:T(8,128)(2,1)} %dy_ref.5, f32[4,16,512]{2,1,0:T(8,128)} %get-tuple-element.29.cum_ref, ...), custom_call_target="tpu_custom_call" | custom-call | flops 12000000000 | bytes 7000000 | tf_op jit(solution)/shard_map/outputs/pallas_call | solution.py:527
  108.4 9.3 %all-to-all-done.2.in_ref = f32[16,160,128]{2,1,0:T(8,128)S(1)} async-done(((f32[16,160,128]{2,1,0:T(8,128)}), f32[16,160,128]{2,1,0:T(8,128)S(1)}, u32[]{:S(2)}, u32[]{:S(2)}) %all-to-all-start.2) | async-done | bytes 1310752 | tf_op jit(solution)/shard_map/all_to_all | solution.py:684
  117.8 0.6 plane_total.1.own_ref
  118.4 0.1 collective-permute-start.4
  118.5 1.6 %collective-permute-start.5 = (f32[160,128]{1,0:T(8,128)S(1)}, f32[160,128]{1,0:T(8,128)S(1)}, u32[]{:S(2)}, u32[]{:S(2)}) collective-permute-start(f32[160,128]{1,0:T(8,128)S(1)} %plane_total.1.own_ref), channel_id=1, source_target_pairs={{0,64},{32,96},{64,0},{96,32},{1,65},{33,97},{65,1},{97,33},{2,66}... | collective-permute-start | bytes 245768 | tf_op jit(solution)/shard_map/ppermute | solution.py:626
  120.1 1.1 collective-permute-start.6
  121.1 2.6 %collective-permute-done.4.back1_ref = f32[160,128]{1,0:T(8,128)S(1)} collective-permute-done((f32[160,128]{1,0:T(8,128)S(1)}, f32[160,128]{1,0:T(8,128)S(1)}, u32[]{:S(2)}, u32[]{:S(2)}) %collective-permute-start.4) | collective-permute-done | bytes 81952 | tf_op jit(solution)/shard_map/ppermute | solution.py:626
  123.7 0.3 collective-permute-done.5.back2_ref
  124.0 0.7 collective-permute-done.6.back3_ref
  124.7 1.2 chips_total.1
  125.9 3.9 %all-to-all-start.3 = ((f32[16,160,128]{2,1,0:T(8,128)}), f32[16,160,128]{2,1,0:T(8,128)S(1)}, u32[]{:S(2)}, u32[]{:S(2)}) async-start(f32[16,160,128]{2,1,0:T(8,128)} %get-tuple-element.50), calls=%async_computation.3 | async-start | bytes 2621440 | tf_op jit(solution)/shard_map/all_to_all | solution.py:684
  129.9 11.4 %outputs.3 = (bf16[512,2560]{1,0:T(8,128)(2,1)}, bf16[512,2560]{1,0:T(8,128)(2,1)}, s32[1]{0:T(128)}) custom-call(s32[1]{0:T(128)} %get-tuple-element.44.c_ref, bf16[512,256]{1,0:T(8,128)(2,1)} %get-tuple-element.28.bc_ref, bf16[512,2560]{1,0:T(8,128)(2,1)} %x_ref.5, bf16[512,2560]{1,0:T(8,128)(2,1)} %dy_ref.5, ...), custom_call_target="tpu_custom_call", output_to_operand_aliasing={{0}: (9, {}), {1}: (10, {})} | custom-call | flops 12000000000 | bytes 7000000 | tf_op jit(solution)/shard_map/outputs/pallas_call | solution.py:527
  141.3 5.8 %all-to-all-done.3 = f32[16,160,128]{2,1,0:T(8,128)S(1)} async-done(((f32[16,160,128]{2,1,0:T(8,128)}), f32[16,160,128]{2,1,0:T(8,128)S(1)}, u32[]{:S(2)}, u32[]{:S(2)}) %all-to-all-start.3) | async-done | bytes 1310752 | tf_op jit(solution)/shard_map/all_to_all | solution.py:684
  147.1 1.3 hold.1
  148.4 3.8 %collective-permute-start.7 = (f32[2,1280,128]{2,1,0:T(8,128)S(1)}, f32[2,1280,128]{2,1,0:T(8,128)S(1)}, u32[]{:S(2)}, u32[]{:S(2)}) collective-permute-start(f32[2,1280,128]{2,1,0:T(8,128)S(1)} %get-tuple-element.51.half_ref), channel_id=1, source_target_pairs={{0,1},{1,0},{2,3},{3,2},{4,5},{5,4},{6,7},{7,6},{8,9},{9,8},{10,11... | collective-permute-start | bytes 3932168 | tf_op jit(solution)/shard_map/ppermute | solution.py:680
  152.1 1.9 %place.2.refs_0_ = f32[2560,256]{1,0:T(8,128)} custom-call(s32[1]{0:T(128)} %get-tuple-element.52.c_ref, f32[2,1280,128]{2,1,0:T(8,128)S(1)} %get-tuple-element.51.half_ref), custom_call_target="tpu_custom_call" | custom-call | tf_op jit(solution)/shard_map/place/pallas_call | solution.py:663
  154.1 0.7 collective-permute-done.7.half_ref
  154.8 1.2 place.3
Async XLA Ops:
  10.0 4.7 %collective-permute-start = (f32[64,48,128]{2,1,0:T(8,128)}, f32[64,48,128]{2,1,0:T(8,128)S(1)}, u32[]{:S(2)}, u32[]{:S(2)}) collective-permute-start(f32[64,48,128]{2,1,0:T(8,128)} %get-tuple-element.32), channel_id=1, source_target_pairs={{0,1},{1,0},{2,3},{3,2},{4,5},{5,4},{6,7},{7,6},{8,9},{9,8},{10,11... | collective-permute-start | bytes 4718600 | tf_op jit(solution)/shard_map/ppermute | solution.py:680
  14.8 1.4 copy-start.2
  17.5 34.0 %all-to-all-start = ((f32[64,48,128]{2,1,0:T(8,128)}), f32[64,48,128]{2,1,0:T(8,128)S(1)}, u32[]{:S(2)}, u32[]{:S(2)}) async-start(f32[64,48,128]{2,1,0:T(8,128)} %chip_sum.1.after_ref), calls=%async_computation | async-start | bytes 3145728 | tf_op jit(solution)/shard_map/all_to_all | solution.py:684
  53.6 24.3 %all-to-all-start.1 = ((f32[64,40,128]{2,1,0:T(8,128)}), f32[64,40,128]{2,1,0:T(8,128)S(1)}, u32[]{:S(2)}, u32[]{:S(2)}) async-start(f32[64,40,128]{2,1,0:T(8,128)} %scan_chips.1), calls=%async_computation.1 | async-start | bytes 2621440 | tf_op jit(solution)/shard_map/all_to_all | solution.py:684
  59.1 25.0 %collective-permute-start.2 = (f32[64,48,128]{2,1,0:T(8,128)}, f32[64,48,128]{2,1,0:T(8,128)S(1)}, u32[]{:S(2)}, u32[]{:S(2)}) collective-permute-start(f32[64,48,128]{2,1,0:T(8,128)} %get-tuple-element.31.mine_ref), channel_id=1, source_target_pairs={{0,1},{1,0},{2,3},{3,2},{4,5},{5,4},{6,7},{7,6},{8,9},{9,8},{10,11... | collective-permute-start | bytes 4718600 | tf_op jit(solution)/shard_map/ppermute | solution.py:680
  77.8 6.3 %collective-permute-start.1 = (f32[64,40,128]{2,1,0:T(8,128)S(1)}, f32[64,40,128]{2,1,0:T(8,128)S(1)}, u32[]{:S(2)}, u32[]{:S(2)}) collective-permute-start(f32[64,40,128]{2,1,0:T(8,128)S(1)} %all-to-all-done.1.came_ref), channel_id=1, source_target_pairs={{0,1},{1,0},{2,3},{3,2},{4,5},{5,4},{6,7},{7,6},{8,9},{9,8},{10,11... | collective-permute-start | bytes 3932168 | tf_op jit(solution)/shard_map/ppermute | solution.py:680
  81.5 1.7 %copy-start = (bf16[512,2560]{1,0:T(8,128)(2,1)S(1)}, bf16[512,2560]{1,0:T(8,128)(2,1)}, u32[]{:S(2)}) copy-start(bf16[512,2560]{1,0:T(8,128)(2,1)} %get-tuple-element.33.w_ref) | copy-start | bytes 7864324
  83.2 1.7 %copy-start.1 = (bf16[512,2560]{1,0:T(8,128)(2,1)S(1)}, bf16[512,2560]{1,0:T(8,128)(2,1)}, u32[]{:S(2)}) copy-start(bf16[512,2560]{1,0:T(8,128)(2,1)} %get-tuple-element.36.wother_ref) | copy-start | bytes 7864324
  83.2 1.9 %copy-start.3 = (f32[512,256]{1,0:T(8,128)S(1)}, f32[512,256]{1,0:T(8,128)}, u32[]{:S(2)}) copy-start(f32[512,256]{1,0:T(8,128)} %get-tuple-element.37.dbc_ref) | copy-start | bytes 1572868
  84.1 4.7 %copy-start.4 = (bf16[128,2560]{1,0:T(8,128)(2,1)}, bf16[128,2560]{1,0:T(8,128)(2,1)S(1)}, u32[]{:S(2)}) copy-start(bf16[128,2560]{1,0:T(8,128)(2,1)S(1)} %get-tuple-element.41.smine_ref) | copy-start | bytes 1966084
  88.8 4.2 %copy-start.5 = (bf16[128,2560]{1,0:T(8,128)(2,1)}, bf16[128,2560]{1,0:T(8,128)(2,1)S(1)}, u32[]{:S(2)}) copy-start(bf16[128,2560]{1,0:T(8,128)(2,1)S(1)} %get-tuple-element.42.sother_ref) | copy-start | bytes 1966084
  88.9 3.1 %collective-permute-start.3 = (f32[2,1280,128]{2,1,0:T(8,128)S(1)}, f32[2,1280,128]{2,1,0:T(8,128)S(1)}, u32[]{:S(2)}, u32[]{:S(2)}) collective-permute-start(f32[2,1280,128]{2,1,0:T(8,128)S(1)} %get-tuple-element.40), channel_id=1, source_target_pairs={{0,1},{1,0},{2,3},{3,2},{4,5},{5,4},{6,7},{7,6},{8,9},{9,8},{10,11... | collective-permute-start | bytes 3932168 | tf_op jit(solution)/shard_map/ppermute | solution.py:680
  93.1 3.7 %copy-start.6 = (f32[40]{0:T(128)S(1)}, f32[40]{0:T(128)}, u32[]{:S(2)}) copy-start(f32[40]{0:T(128)} %param.12) | copy-start | bytes 484
  93.1 24.6 %all-to-all-start.2 = ((f32[16,160,128]{2,1,0:T(8,128)}), f32[16,160,128]{2,1,0:T(8,128)S(1)}, u32[]{:S(2)}, u32[]{:S(2)}) async-start(f32[16,160,128]{2,1,0:T(8,128)} %bitcast.3), calls=%async_computation.2 | async-start | bytes 2621440 | tf_op jit(solution)/shard_map/all_to_all | solution.py:684
  118.4 5.3 %collective-permute-start.4 = (f32[160,128]{1,0:T(8,128)S(1)}, f32[160,128]{1,0:T(8,128)S(1)}, u32[]{:S(2)}, u32[]{:S(2)}) collective-permute-start(f32[160,128]{1,0:T(8,128)S(1)} %plane_total.1.own_ref), channel_id=1, source_target_pairs={{0,32},{32,64},{64,96},{96,0},{1,33},{33,65},{65,97},{97,1},{2,34}... | collective-permute-start | bytes 245768 | tf_op jit(solution)/shard_map/ppermute | solution.py:626
  118.5 5.5 %collective-permute-start.5 = (f32[160,128]{1,0:T(8,128)S(1)}, f32[160,128]{1,0:T(8,128)S(1)}, u32[]{:S(2)}, u32[]{:S(2)}) collective-permute-start(f32[160,128]{1,0:T(8,128)S(1)} %plane_total.1.own_ref), channel_id=1, source_target_pairs={{0,64},{32,96},{64,0},{96,32},{1,65},{33,97},{65,1},{97,33},{2,66}... | collective-permute-start | bytes 245768 | tf_op jit(solution)/shard_map/ppermute | solution.py:626
  120.1 4.6 %collective-permute-start.6 = (f32[160,128]{1,0:T(8,128)S(1)}, f32[160,128]{1,0:T(8,128)S(1)}, u32[]{:S(2)}, u32[]{:S(2)}) collective-permute-start(f32[160,128]{1,0:T(8,128)S(1)} %plane_total.1.own_ref), channel_id=1, source_target_pairs={{0,96},{32,0},{64,32},{96,64},{1,97},{33,1},{65,33},{97,65},{2,98}... | collective-permute-start | bytes 245768 | tf_op jit(solution)/shard_map/ppermute | solution.py:626
  125.9 21.1 %all-to-all-start.3 = ((f32[16,160,128]{2,1,0:T(8,128)}), f32[16,160,128]{2,1,0:T(8,128)S(1)}, u32[]{:S(2)}, u32[]{:S(2)}) async-start(f32[16,160,128]{2,1,0:T(8,128)} %get-tuple-element.50), calls=%async_computation.3 | async-start | bytes 2621440 | tf_op jit(solution)/shard_map/all_to_all | solution.py:684
  148.4 6.4 %collective-permute-start.7 = (f32[2,1280,128]{2,1,0:T(8,128)S(1)}, f32[2,1280,128]{2,1,0:T(8,128)S(1)}, u32[]{:S(2)}, u32[]{:S(2)}) collective-permute-start(f32[2,1280,128]{2,1,0:T(8,128)S(1)} %get-tuple-element.51.half_ref), channel_id=1, source_target_pairs={{0,1},{1,0},{2,3},{3,2},{4,5},{5,4},{6,7},{7,6},{8,9},{9,8},{10,11... | collective-permute-start | bytes 3932168 | tf_op jit(solution)/shard_map/ppermute | solution.py:680

commit v3 on v2

--- a/solution.py
+++ b/solution.py
@@ -26,8 +26,7 @@
 STATE_ROWS = 8 * GT
 ROWS = 48
 HALF_D = D // 2
-PLANE = 16
-GW_ROWS = 2 * HALF_D // PLANE
+GW_ROWS = 2 * HALF_D // CHIPS
 KC = 5
 KL = D // KC
 LARGE = 56 << 20
@@ -122,7 +121,9 @@
     rest = step - p1.astype(F32)
     p2 = rest.astype(BF16)
     p3 = (rest - p2.astype(F32)).astype(BF16)
-    cum = mm(p1, upper) + mm(p2, upper) + mm(p3, upper)
+    sums = mm(jnp.concatenate([p1, p2, p3, jnp.zeros((8, T), BF16)]), upper)
+    cum = sums[0:H] + sums[H : 2 * H] + sums[2 * H : 3 * H]
+    by_token = jnp.concatenate([cum, jnp.zeros((128 - H, T), F32)]).T
     stores = []
 
     def send(src, dst, sem):
@@ -131,8 +132,7 @@
 
     for q in range(G):
         cum_scr[q, 0:GH, :] = cum[GH * q : GH * (q + 1), :]
-        full = jnp.concatenate([cum_scr[q], jnp.zeros((112, T), F32)])
-        cumt_scr[q] = full.T
+        cumt_scr[q] = by_token if q == 0 else pltpu.roll(by_token, 128 - GH * q, 1)
     send(cum_scr, cum_hbm, small_sem.at[1])
     send(cumt_scr, cumt_hbm, small_sem.at[2])
     for q in range(KC):
@@ -591,48 +591,22 @@
     )(a, b)
 
 
-def plane_kernel(in_ref, after_ref, out_ref):
-    out_ref[...] = jnp.sum(in_ref[...], axis=0)
-
-
-def plane_total(parts, after):
-    return pl.pallas_call(
-        plane_kernel,
-        in_specs=[WHOLE, IN_SMEM],
-        out_specs=WHOLE,
-        out_shape=jax.ShapeDtypeStruct((GW_ROWS, 128), F32),
-        compiler_params=pltpu.CompilerParams(vmem_limit_bytes=SMALL),
-        name="plane_total",
-    )(parts, after)
-
-
-def chips_kernel(c_ref, z_ref, own_ref, back1_ref, back2_ref, back3_ref, out_ref, token_ref):
-    z = z_ref[0]
-    held = [own_ref[...], back1_ref[...], back2_ref[...], back3_ref[...]]
-    total = None
-    for plane in range(4):
-        behind = jnp.bitwise_and(z - plane, 3)
-        part = held[3]
-        for k in range(3):
-            part = jnp.where(behind == k, held[k], part)
-        total = part if total is None else total + part
-    for k in range(PLANE):
+def total_kernel(c_ref, in_ref, out_ref, token_ref):
+    total = jnp.sum(in_ref[...], axis=0)
+    for k in range(CHIPS):
         out_ref[k] = total
     token_ref[0] = c_ref[0]
 
 
-def chips_total(core, z, own):
-    others = [
-        lax.ppermute(own, "z", [(i, (i + k) % 4) for i in range(4)]) for k in (1, 2, 3)
-    ]
-    return pl.pallas_call(
-        chips_kernel,
-        in_specs=[IN_SMEM] * 2 + [WHOLE] * 4,
+def chip_total(core, parts):
+    return pl.pallas_call(
+        total_kernel,
+        in_specs=[IN_SMEM, WHOLE],
         out_specs=[WHOLE, IN_SMEM],
-        out_shape=[jax.ShapeDtypeStruct((PLANE, GW_ROWS, 128), F32), TOKEN],
+        out_shape=[jax.ShapeDtypeStruct((CHIPS, GW_ROWS, 128), F32), TOKEN],
         compiler_params=pltpu.CompilerParams(vmem_limit_bytes=SMALL),
-        name="chips_total",
-    )(core, z, own, *others)
+        name="chip_total",
+    )(core, parts)
 
 
 def hold_kernel(c_ref, in_ref, out_ref, token_ref):
@@ -680,8 +654,8 @@
     return lax.ppermute(v, "c", [(0, 1), (1, 0)])
 
 
-def exchange(v, axes=CHIP_AXES):
-    return lax.all_to_all(v, axes, 0, 0, tiled=True)
+def exchange(v):
+    return lax.all_to_all(v, CHIP_AXES, 0, 0, tiled=True)
 
 
 def shards(hidden, w_bc, ssm_in, codes, rates, skip, grad_out):
@@ -702,12 +676,11 @@
         core, acc_mine, w_other, swap(came), theirs, dbc, turned
     )
     part = pair_add(gw_mine, swap(gw_other))
-    sums = exchange(part.reshape(PLANE, GW_ROWS, 128), ("x", "y"))
+    sums = exchange(part.reshape(CHIPS, GW_ROWS, 128))
     pieces = (bc, ssm_in, grad_out, cum, cumt, skip_row, s_mine, s_other)
-    mixed, gradx, done = outputs(core, *pieces, 0, [part])
-    z = lax.axis_index("z").astype(jnp.int32).reshape(1)
-    total, core_after = chips_total(core, z, plane_total(sums, done))
-    half = exchange(total, ("x", "y")).reshape(2, HALF_D, 128)
+    mixed, gradx, core_after = outputs(core, *pieces, 0, [part])
+    total, core_after = chip_total(core_after, sums)
+    half = exchange(total).reshape(2, HALF_D, 128)
     mixed, gradx, core_after = outputs(core_after, *pieces, G // 2, [mixed, gradx])
     half, core_after = hold(core_after, half)
     grad_w = place(1 - core, swap(half), place(core_after, half, None))

time: 157 us -> 154 us (0.981)
  waiting for transfers between devices: 50.8 us -> 48.3 us
    ppermute x3 -> x0, waiting for transfers between devices: 3.57 us -> none  [chips_total(): lax.ppermute(own, 'z', [(i, (i + k) % 4) for i in range(4)])]
    ppermute x3 -> x0, starting transfers between devices: 2.74 us -> none  [chips_total(): lax.ppermute(own, 'z', [(i, (i + k) % 4) for i in range(4)])]
    all_to_all x4, starting transfers between devices: 24.4 us -> 27.1 us  [exchange(): return lax.all_to_all(v, CHIP_AXES, 0, 0, tiled=True)]
  transfers between devices with their start and end apart: 12 -> 9, of which waited for: 10 -> 7; matrix products, arithmetic and copies ran while one was open for 0% -> 0% of each run, Pallas kernels for 25% -> 25%
where the time goes in v3:
time: 154 us; the launch traced here: 153 us
  Pallas kernels  60.7 us (39%)
  waiting for transfers between devices  48.3 us (31%)
  starting transfers between devices  38.3 us (25%)
  local copies, waits for them, and re-layouts  4.89 us (3%)
    all_to_all x4, waiting for transfers between devices, exchange(): return lax.all_to_all(v, CHIP_AXES, 0, 0, tiled=True)  41.2 us
    all_to_all x4, starting transfers between devices, exchange(): return lax.all_to_all(v, CHIP_AXES, 0, 0, tiled=True)  27.1 us
    pallas_call x2, Pallas kernels, outputs(): pl.pallas_call(outputs_kernel, grid=(G // 2,), in_specs=[IN_SMEM, full_sp...  22.3 us
    pallas_call x1, Pallas kernels, pairs(): pl.pallas_call(pairs_kernel, grid=(G,), in_specs=[pl.BlockSpec(memory_spa...  14 us
    ppermute x5, starting transfers between devices, swap(): return lax.ppermute(v, 'c', [(0, 1), (1, 0)])  11.3 us
    pallas_call x1, Pallas kernels, pre(): pl.pallas_call(pre_kernel, in_specs=[pl.BlockSpec(memory_space=pltpu.SMEM...  9.34 us
    ppermute x5, waiting for transfers between devices, swap(): return lax.ppermute(v, 'c', [(0, 1), (1, 0)])  7.09 us
    unnamed x14, local copies, waits for them, and re-layouts  4.13 us
  transfers between devices with their start and end apart: 9, of which 7 were waited for; matrix products, arithmetic and copies ran while one was open for 0% of the time, Pallas kernels for 25%

profile of v3, /device:TPU:1, one launch (start us, length us, event | category | flops | bytes accessed | tf_op | source)
XLA Modules:
  0.0 153.0 jit_solution(12248041058132504560)
XLA Ops:
  0.6 9.3 %pre.1 = (bf16[512,256]{1,0:T(8,128)(2,1)}, f32[4,16,512]{2,1,0:T(8,128)}, f32[4,512,128]{2,1,0:T(8,128)}, f32[64,48,128]{2,1,0:T(8,128)}, f32[64,48,128]{2,1,0:T(8,128)}) custom-call(s32[1]{0:T(128)} %bitcast.c_ref, f32[1,40]{1,0:T(1,128)} %bitcast.5, bf16[512,2560]{1,0:T(8,128)(2,1)} %hidden_ref.1, bf16[2560,256]{1,0:T(8,128)(2,1)} %w_hbm.1, ...), custom_call_target="tpu_custom_call" | custom-call | flops 2000000000 | bytes 13000000 | tf_op jit(solution)/shard_map/pre/pallas_call | solution.py:177
  10.0 1.5 collective-permute-start
  11.5 3.2 %collective-permute-done.got_ref = f32[64,48,128]{2,1,0:T(8,128)S(1)} collective-permute-done((f32[64,48,128]{2,1,0:T(8,128)}, f32[64,48,128]{2,1,0:T(8,128)S(1)}, u32[]{:S(2)}, u32[]{:S(2)}) %collective-permute-start) | collective-permute-done | bytes 1572896 | tf_op jit(solution)/shard_map/ppermute | solution.py:654
  14.7 0.0 copy-start.2
  14.7 1.4 copy-done.2
  16.1 1.4 chip_sum.1.after_ref
  17.5 11.2 %all-to-all-start = ((f32[64,48,128]{2,1,0:T(8,128)}), f32[64,48,128]{2,1,0:T(8,128)S(1)}, u32[]{:S(2)}, u32[]{:S(2)}) async-start(f32[64,48,128]{2,1,0:T(8,128)} %chip_sum.1.after_ref), calls=%async_computation | async-start | bytes 3145728 | tf_op jit(solution)/shard_map/all_to_all | solution.py:658
  28.7 14.0 %pairs.1 = (bf16[512,2560]{1,0:T(8,128)(2,1)}, bf16[512,2560]{1,0:T(8,128)(2,1)}, f32[512,256]{1,0:T(8,128)}, bf16[2560,512]{1,0:T(8,128)(2,1)}, s32[1]{0:T(128)}) custom-call(s32[1]{0:T(128)} %bitcast.c_ref, bf16[512,256]{1,0:T(8,128)(2,1)} %get-tuple-element.28.bc_ref, bf16[512,2560]{1,0:T(8,128)(2,1)} %x_ref.5, bf16[512,2560]{1,0:T(8,128)(2,1)} %dy_ref.5, ...), custom_call_target="tpu_custom_call" | custom-call | flops 20000000000 | bytes 16000000 | tf_op jit(solution)/shard_map/pairs/pallas_call | solution.py:337
  42.7 8.8 %all-to-all-done.in_ref = f32[64,48,128]{2,1,0:T(8,128)S(1)} async-done(((f32[64,48,128]{2,1,0:T(8,128)}), f32[64,48,128]{2,1,0:T(8,128)S(1)}, u32[]{:S(2)}, u32[]{:S(2)}) %all-to-all-start) | async-done | bytes 1572896 | tf_op jit(solution)/shard_map/all_to_all | solution.py:658
  51.5 1.9 %scan_chips.1 = f32[64,40,128]{2,1,0:T(8,128)} custom-call(s32[1]{0:T(128)} %bitcast.c_ref, f32[64,48,128]{2,1,0:T(8,128)S(1)} %all-to-all-done.in_ref, s32[1]{0:T(128)} %get-tuple-element.34.after_ref), custom_call_target="tpu_custom_call" | custom-call | tf_op jit(solution)/shard_map/scan_chips/pallas_call | solution.py:245
  53.4 5.5 %all-to-all-start.1 = ((f32[64,40,128]{2,1,0:T(8,128)}), f32[64,40,128]{2,1,0:T(8,128)S(1)}, u32[]{:S(2)}, u32[]{:S(2)}) async-start(f32[64,40,128]{2,1,0:T(8,128)} %scan_chips.1), calls=%async_computation.1 | async-start | bytes 2621440 | tf_op jit(solution)/shard_map/all_to_all | solution.py:658
  59.0 2.4 %collective-permute-start.2 = (f32[64,48,128]{2,1,0:T(8,128)}, f32[64,48,128]{2,1,0:T(8,128)S(1)}, u32[]{:S(2)}, u32[]{:S(2)}) collective-permute-start(f32[64,48,128]{2,1,0:T(8,128)} %get-tuple-element.31.mine_ref), channel_id=1, source_target_pairs={{0,1},{1,0},{2,3},{3,2},{4,5},{5,4},{6,7},{7,6},{8,9},{9,8},{10,11... | collective-permute-start | bytes 4718600 | tf_op jit(solution)/shard_map/ppermute | solution.py:654
  61.4 16.3 %all-to-all-done.1.came_ref = f32[64,40,128]{2,1,0:T(8,128)S(1)} async-done(((f32[64,40,128]{2,1,0:T(8,128)}), f32[64,40,128]{2,1,0:T(8,128)S(1)}, u32[]{:S(2)}, u32[]{:S(2)}) %all-to-all-start.1) | async-done | bytes 1310752 | tf_op jit(solution)/shard_map/all_to_all | solution.py:658
  77.7 3.7 %collective-permute-start.1 = (f32[64,40,128]{2,1,0:T(8,128)S(1)}, f32[64,40,128]{2,1,0:T(8,128)S(1)}, u32[]{:S(2)}, u32[]{:S(2)}) collective-permute-start(f32[64,40,128]{2,1,0:T(8,128)S(1)} %all-to-all-done.1.came_ref), channel_id=1, source_target_pairs={{0,1},{1,0},{2,3},{3,2},{4,5},{5,4},{6,7},{7,6},{8,9},{9,8},{10,11... | collective-permute-start | bytes 3932168 | tf_op jit(solution)/shard_map/ppermute | solution.py:654
  81.3 0.0 copy-start
  81.4 1.7 %copy-done = bf16[512,2560]{1,0:T(8,128)(2,1)S(1)} copy-done((bf16[512,2560]{1,0:T(8,128)(2,1)S(1)}, bf16[512,2560]{1,0:T(8,128)(2,1)}, u32[]{:S(2)}) %copy-start) | copy-done | bytes 2621464
  83.1 0.0 copy-start.1
  83.1 0.0 copy-start.3
  83.1 0.9 carry.1
  84.0 0.0 copy-start.4
  84.0 0.0 collective-permute-done.2.theirs_ref
  84.0 0.0 collective-permute-done.1.came_ref
  84.0 0.8 copy-done.1
  84.8 0.2 copy-done.3
  85.0 3.7 %weight_part.1 = (f32[2,1280,128]{2,1,0:T(8,128)S(1)}, f32[2,1280,128]{2,1,0:T(8,128)S(1)}, bf16[128,2560]{1,0:T(8,128)(2,1)S(1)}) custom-call(s32[1]{0:T(128)} %bitcast.c_ref, f32[512,128]{1,0:T(8,128)S(1)} %get-tuple-element.36.accmine_ref, bf16[512,2560]{1,0:T(8,128)(2,1)S(1)} %copy-done.1, f32[64,40,128]{2,1,0:T(8,128)S(1)} %collective-permute-done.1.came_ref, ...), custom_call_target="tpu_custom_call" | custom-call | flops 2000000000 | bytes 12000000 | tf_op jit(solution)/shard_map/weight_part/pallas_call | solution.py:450
  88.7 0.0 copy-done.4
  88.7 0.0 copy-start.5
  88.7 0.1 collective-permute-start.3
  88.8 3.0 %collective-permute-done.3.b_ref = f32[2,1280,128]{2,1,0:T(8,128)S(1)} collective-permute-done((f32[2,1280,128]{2,1,0:T(8,128)S(1)}, f32[2,1280,128]{2,1,0:T(8,128)S(1)}, u32[]{:S(2)}, u32[]{:S(2)}) %collective-permute-start.3) | collective-permute-done | bytes 1310752 | tf_op jit(solution)/shard_map/ppermute | solution.py:654
  91.8 1.1 pair_add.1.refs_0_
  92.9 0.0 copy-done.5
  93.0 0.0 copy-start.6
  93.0 4.7 %all-to-all-start.2 = ((f32[64,40,128]{2,1,0:T(8,128)}), f32[64,40,128]{2,1,0:T(8,128)S(1)}, u32[]{:S(2)}, u32[]{:S(2)}) async-start(f32[64,40,128]{2,1,0:T(8,128)} %bitcast.2), calls=%async_computation.2 | async-start | bytes 2621440 | tf_op jit(solution)/shard_map/all_to_all | solution.py:658
  97.7 0.0 copy-done.6
  97.7 0.1 broadcast_in_dim.7
  97.8 0.7 broadcast_in_dim_reshape.3.skip_ref
  98.5 10.8 %outputs.2 = (bf16[512,2560]{1,0:T(8,128)(2,1)}, bf16[512,2560]{1,0:T(8,128)(2,1)}, s32[1]{0:T(128)}) custom-call(s32[1]{0:T(128)} %bitcast.c_ref, bf16[512,256]{1,0:T(8,128)(2,1)} %get-tuple-element.28.bc_ref, bf16[512,2560]{1,0:T(8,128)(2,1)} %x_ref.5, bf16[512,2560]{1,0:T(8,128)(2,1)} %dy_ref.5, f32[4,16,512]{2,1,0:T(8,128)} %get-tuple-element.29.cum_ref, ...), custom_call_target="tpu_custom_call" | custom-call | flops 12000000000 | bytes 7000000 | tf_op jit(solution)/shard_map/outputs/pallas_call | solution.py:527
  109.3 8.9 %all-to-all-done.2.in_ref = f32[64,40,128]{2,1,0:T(8,128)S(1)} async-done(((f32[64,40,128]{2,1,0:T(8,128)}), f32[64,40,128]{2,1,0:T(8,128)S(1)}, u32[]{:S(2)}, u32[]{:S(2)}) %all-to-all-start.2) | async-done | bytes 1310752 | tf_op jit(solution)/shard_map/all_to_all | solution.py:658
  118.2 1.8 %chip_total.1 = (f32[64,40,128]{2,1,0:T(8,128)}, s32[1]{0:T(128)}) custom-call(s32[1]{0:T(128)} %get-tuple-element.43.c_ref, f32[64,40,128]{2,1,0:T(8,128)S(1)} %all-to-all-done.2.in_ref), custom_call_target="tpu_custom_call" | custom-call | tf_op jit(solution)/shard_map/chip_total/pallas_call | solution.py:602
  120.1 5.6 %all-to-all-start.3 = ((f32[64,40,128]{2,1,0:T(8,128)}), f32[64,40,128]{2,1,0:T(8,128)S(1)}, u32[]{:S(2)}, u32[]{:S(2)}) async-start(f32[64,40,128]{2,1,0:T(8,128)} %get-tuple-element.50), calls=%async_computation.3 | async-start | bytes 2621440 | tf_op jit(solution)/shard_map/all_to_all | solution.py:658
  125.7 11.5 %outputs.3 = (bf16[512,2560]{1,0:T(8,128)(2,1)}, bf16[512,2560]{1,0:T(8,128)(2,1)}, s32[1]{0:T(128)}) custom-call(s32[1]{0:T(128)} %get-tuple-element.44.c_ref, bf16[512,256]{1,0:T(8,128)(2,1)} %get-tuple-element.28.bc_ref, bf16[512,2560]{1,0:T(8,128)(2,1)} %x_ref.5, bf16[512,2560]{1,0:T(8,128)(2,1)} %dy_ref.5, ...), custom_call_target="tpu_custom_call", output_to_operand_aliasing={{0}: (9, {}), {1}: (10, {})} | custom-call | flops 12000000000 | bytes 7000000 | tf_op jit(solution)/shard_map/outputs/pallas_call | solution.py:527
  137.1 7.2 %all-to-all-done.3 = f32[64,40,128]{2,1,0:T(8,128)S(1)} async-done(((f32[64,40,128]{2,1,0:T(8,128)}), f32[64,40,128]{2,1,0:T(8,128)S(1)}, u32[]{:S(2)}, u32[]{:S(2)}) %all-to-all-start.3) | async-done | bytes 1310752 | tf_op jit(solution)/shard_map/all_to_all | solution.py:658
  144.3 1.2 hold.1
  145.6 3.6 %collective-permute-start.4 = (f32[2,1280,128]{2,1,0:T(8,128)S(1)}, f32[2,1280,128]{2,1,0:T(8,128)S(1)}, u32[]{:S(2)}, u32[]{:S(2)}) collective-permute-start(f32[2,1280,128]{2,1,0:T(8,128)S(1)} %get-tuple-element.51.half_ref), channel_id=1, source_target_pairs={{0,1},{1,0},{2,3},{3,2},{4,5},{5,4},{6,7},{7,6},{8,9},{9,8},{10,11... | collective-permute-start | bytes 3932168 | tf_op jit(solution)/shard_map/ppermute | solution.py:654
  149.1 1.8 %place.2.refs_0_ = f32[2560,256]{1,0:T(8,128)} custom-call(s32[1]{0:T(128)} %get-tuple-element.52.c_ref, f32[2,1280,128]{2,1,0:T(8,128)S(1)} %get-tuple-element.51.half_ref), custom_call_target="tpu_custom_call" | custom-call | tf_op jit(solution)/shard_map/place/pallas_call | solution.py:637
  151.0 0.8 collective-permute-done.4.half_ref
  151.8 1.2 place.3
Async XLA Ops:
  10.0 4.8 %collective-permute-start = (f32[64,48,128]{2,1,0:T(8,128)}, f32[64,48,128]{2,1,0:T(8,128)S(1)}, u32[]{:S(2)}, u32[]{:S(2)}) collective-permute-start(f32[64,48,128]{2,1,0:T(8,128)} %get-tuple-element.32), channel_id=1, source_target_pairs={{0,1},{1,0},{2,3},{3,2},{4,5},{5,4},{6,7},{7,6},{8,9},{9,8},{10,11... | collective-permute-start | bytes 4718600 | tf_op jit(solution)/shard_map/ppermute | solution.py:654
  14.7 1.4 copy-start.2
  17.5 34.0 %all-to-all-start = ((f32[64,48,128]{2,1,0:T(8,128)}), f32[64,48,128]{2,1,0:T(8,128)S(1)}, u32[]{:S(2)}, u32[]{:S(2)}) async-start(f32[64,48,128]{2,1,0:T(8,128)} %chip_sum.1.after_ref), calls=%async_computation | async-start | bytes 3145728 | tf_op jit(solution)/shard_map/all_to_all | solution.py:658
  53.4 24.3 %all-to-all-start.1 = ((f32[64,40,128]{2,1,0:T(8,128)}), f32[64,40,128]{2,1,0:T(8,128)S(1)}, u32[]{:S(2)}, u32[]{:S(2)}) async-start(f32[64,40,128]{2,1,0:T(8,128)} %scan_chips.1), calls=%async_computation.1 | async-start | bytes 2621440 | tf_op jit(solution)/shard_map/all_to_all | solution.py:658
  59.0 25.0 %collective-permute-start.2 = (f32[64,48,128]{2,1,0:T(8,128)}, f32[64,48,128]{2,1,0:T(8,128)S(1)}, u32[]{:S(2)}, u32[]{:S(2)}) collective-permute-start(f32[64,48,128]{2,1,0:T(8,128)} %get-tuple-element.31.mine_ref), channel_id=1, source_target_pairs={{0,1},{1,0},{2,3},{3,2},{4,5},{5,4},{6,7},{7,6},{8,9},{9,8},{10,11... | collective-permute-start | bytes 4718600 | tf_op jit(solution)/shard_map/ppermute | solution.py:654
  77.7 6.3 %collective-permute-start.1 = (f32[64,40,128]{2,1,0:T(8,128)S(1)}, f32[64,40,128]{2,1,0:T(8,128)S(1)}, u32[]{:S(2)}, u32[]{:S(2)}) collective-permute-start(f32[64,40,128]{2,1,0:T(8,128)S(1)} %all-to-all-done.1.came_ref), channel_id=1, source_target_pairs={{0,1},{1,0},{2,3},{3,2},{4,5},{5,4},{6,7},{7,6},{8,9},{9,8},{10,11... | collective-permute-start | bytes 3932168 | tf_op jit(solution)/shard_map/ppermute | solution.py:654
  81.3 1.7 %copy-start = (bf16[512,2560]{1,0:T(8,128)(2,1)S(1)}, bf16[512,2560]{1,0:T(8,128)(2,1)}, u32[]{:S(2)}) copy-start(bf16[512,2560]{1,0:T(8,128)(2,1)} %get-tuple-element.33.w_ref) | copy-start | bytes 7864324
  83.1 1.7 %copy-start.1 = (bf16[512,2560]{1,0:T(8,128)(2,1)S(1)}, bf16[512,2560]{1,0:T(8,128)(2,1)}, u32[]{:S(2)}) copy-start(bf16[512,2560]{1,0:T(8,128)(2,1)} %get-tuple-element.37.wother_ref) | copy-start | bytes 7864324
  83.1 1.9 %copy-start.3 = (f32[512,256]{1,0:T(8,128)S(1)}, f32[512,256]{1,0:T(8,128)}, u32[]{:S(2)}) copy-start(f32[512,256]{1,0:T(8,128)} %get-tuple-element.38.dbc_ref) | copy-start | bytes 1572868
  84.0 4.7 %copy-start.4 = (bf16[128,2560]{1,0:T(8,128)(2,1)}, bf16[128,2560]{1,0:T(8,128)(2,1)S(1)}, u32[]{:S(2)}) copy-start(bf16[128,2560]{1,0:T(8,128)(2,1)S(1)} %get-tuple-element.35.smine_ref) | copy-start | bytes 1966084
  88.7 4.2 %copy-start.5 = (bf16[128,2560]{1,0:T(8,128)(2,1)}, bf16[128,2560]{1,0:T(8,128)(2,1)S(1)}, u32[]{:S(2)}) copy-start(bf16[128,2560]{1,0:T(8,128)(2,1)S(1)} %get-tuple-element.40.sother_ref) | copy-start | bytes 1966084
  88.7 3.1 %collective-permute-start.3 = (f32[2,1280,128]{2,1,0:T(8,128)S(1)}, f32[2,1280,128]{2,1,0:T(8,128)S(1)}, u32[]{:S(2)}, u32[]{:S(2)}) collective-permute-start(f32[2,1280,128]{2,1,0:T(8,128)S(1)} %get-tuple-element.42), channel_id=1, source_target_pairs={{0,1},{1,0},{2,3},{3,2},{4,5},{5,4},{6,7},{7,6},{8,9},{9,8},{10,11... | collective-permute-start | bytes 3932168 | tf_op jit(solution)/shard_map/ppermute | solution.py:654
  93.0 4.8 %copy-start.6 = (f32[40]{0:T(128)S(1)}, f32[40]{0:T(128)}, u32[]{:S(2)}) copy-start(f32[40]{0:T(128)} %param.12) | copy-start | bytes 484
  93.0 25.2 %all-to-all-start.2 = ((f32[64,40,128]{2,1,0:T(8,128)}), f32[64,40,128]{2,1,0:T(8,128)S(1)}, u32[]{:S(2)}, u32[]{:S(2)}) async-start(f32[64,40,128]{2,1,0:T(8,128)} %bitcast.2), calls=%async_computation.2 | async-start | bytes 2621440 | tf_op jit(solution)/shard_map/all_to_all | solution.py:658
  120.1 24.3 %all-to-all-start.3 = ((f32[64,40,128]{2,1,0:T(8,128)}), f32[64,40,128]{2,1,0:T(8,128)S(1)}, u32[]{:S(2)}, u32[]{:S(2)}) async-start(f32[64,40,128]{2,1,0:T(8,128)} %get-tuple-element.50), calls=%async_computation.3 | async-start | bytes 2621440 | tf_op jit(solution)/shard_map/all_to_all | solution.py:658
  145.6 6.2 %collective-permute-start.4 = (f32[2,1280,128]{2,1,0:T(8,128)S(1)}, f32[2,1280,128]{2,1,0:T(8,128)S(1)}, u32[]{:S(2)}, u32[]{:S(2)}) collective-permute-start(f32[2,1280,128]{2,1,0:T(8,128)S(1)} %get-tuple-element.51.half_ref), channel_id=1, source_target_pairs={{0,1},{1,0},{2,3},{3,2},{4,5},{5,4},{6,7},{7,6},{8,9},{9,8},{10,11... | collective-permute-start | bytes 3932168 | tf_op jit(solution)/shard_map/ppermute | solution.py:654

commit v4 on v3

--- a/solution.py
+++ b/solution.py
@@ -591,19 +591,31 @@
     )(a, b)
 
 
-def total_kernel(c_ref, in_ref, out_ref, token_ref):
+def total_kernel(c_ref, in_ref, out_hbm, token_ref, scr, sem):
     total = jnp.sum(in_ref[...], axis=0)
-    for k in range(CHIPS):
-        out_ref[k] = total
+    for k in range(NM // 2):
+        scr[k] = total
+    stores = [
+        pltpu.make_async_copy(scr, out_hbm.at[pl.ds(NM // 2 * j, NM // 2)], sem.at[j])
+        for j in range(2 * CHIPS // NM)
+    ]
+    for store in stores:
+        store.start()
     token_ref[0] = c_ref[0]
+    for store in stores:
+        store.wait()
 
 
 def chip_total(core, parts):
     return pl.pallas_call(
         total_kernel,
         in_specs=[IN_SMEM, WHOLE],
-        out_specs=[WHOLE, IN_SMEM],
+        out_specs=[IN_HBM, IN_SMEM],
         out_shape=[jax.ShapeDtypeStruct((CHIPS, GW_ROWS, 128), F32), TOKEN],
+        scratch_shapes=[
+            pltpu.VMEM((NM // 2, GW_ROWS, 128), F32),
+            pltpu.SemaphoreType.DMA((2 * CHIPS // NM,)),
+        ],
         compiler_params=pltpu.CompilerParams(vmem_limit_bytes=SMALL),
         name="chip_total",
     )(core, parts)

time: 154 us -> 154 us (level)
  no operation moved by 1% of the time
where the time goes in v4:
time: 154 us
  Pallas kernels  61.2 us (40%)
  waiting for transfers between devices  48.3 us (31%)
  starting transfers between devices  38.3 us (25%)
  local copies, waits for them, and re-layouts  4.89 us (3%)
    all_to_all x4, waiting for transfers between devices, exchange(): return lax.all_to_all(v, CHIP_AXES, 0, 0, tiled=True)  41.2 us
    all_to_all x4, starting transfers between devices, exchange(): return lax.all_to_all(v, CHIP_AXES, 0, 0, tiled=True)  27.1 us
    pallas_call x2, Pallas kernels, outputs(): pl.pallas_call(outputs_kernel, grid=(G // 2,), in_specs=[IN_SMEM, full_sp...  22.3 us
    pallas_call x1, Pallas kernels, pairs(): pl.pallas_call(pairs_kernel, grid=(G,), in_specs=[pl.BlockSpec(memory_spa...  14 us
    ppermute x5, starting transfers between devices, swap(): return lax.ppermute(v, 'c', [(0, 1), (1, 0)])  11.3 us
    pallas_call x1, Pallas kernels, pre(): pl.pallas_call(pre_kernel, in_specs=[pl.BlockSpec(memory_space=pltpu.SMEM...  9.34 us
    ppermute x5, waiting for transfers between devices, swap(): return lax.ppermute(v, 'c', [(0, 1), (1, 0)])  7.09 us
    unnamed x14, local copies, waits for them, and re-layouts  4.13 us
  transfers between devices with their start and end apart: 9, of which 7 were waited for; matrix products, arithmetic and copies ran while one was open for 0% of the time, Pallas kernels for 25%

profile of v4, /device:TPU:1, one launch (start us, length us, event | category | flops | bytes accessed | tf_op | source)
XLA Modules:
  0.0 153.5 jit_solution(14699537847960637457)
XLA Ops:
  0.6 9.3 %pre.1 = (bf16[512,256]{1,0:T(8,128)(2,1)}, f32[4,16,512]{2,1,0:T(8,128)}, f32[4,512,128]{2,1,0:T(8,128)}, f32[64,48,128]{2,1,0:T(8,128)}, f32[64,48,128]{2,1,0:T(8,128)}) custom-call(s32[1]{0:T(128)} %bitcast.c_ref, f32[1,40]{1,0:T(1,128)} %bitcast.5, bf16[512,2560]{1,0:T(8,128)(2,1)} %hidden_ref.1, bf16[2560,256]{1,0:T(8,128)(2,1)} %w_hbm.1, ...), custom_call_target="tpu_custom_call" | custom-call | flops 2000000000 | bytes 13000000 | tf_op jit(solution)/shard_map/pre/pallas_call | solution.py:177
  10.0 1.5 collective-permute-start
  11.5 3.2 %collective-permute-done.got_ref = f32[64,48,128]{2,1,0:T(8,128)S(1)} collective-permute-done((f32[64,48,128]{2,1,0:T(8,128)}, f32[64,48,128]{2,1,0:T(8,128)S(1)}, u32[]{:S(2)}, u32[]{:S(2)}) %collective-permute-start) | collective-permute-done | bytes 1572896 | tf_op jit(solution)/shard_map/ppermute | solution.py:666
  14.7 0.0 copy-start.2
  14.7 1.4 copy-done.2
  16.1 1.4 chip_sum.1.after_ref
  17.5 11.2 %all-to-all-start = ((f32[64,48,128]{2,1,0:T(8,128)}), f32[64,48,128]{2,1,0:T(8,128)S(1)}, u32[]{:S(2)}, u32[]{:S(2)}) async-start(f32[64,48,128]{2,1,0:T(8,128)} %chip_sum.1.after_ref), calls=%async_computation | async-start | bytes 3145728 | tf_op jit(solution)/shard_map/all_to_all | solution.py:670
  28.7 14.0 %pairs.1 = (bf16[512,2560]{1,0:T(8,128)(2,1)}, bf16[512,2560]{1,0:T(8,128)(2,1)}, f32[512,256]{1,0:T(8,128)}, bf16[2560,512]{1,0:T(8,128)(2,1)}, s32[1]{0:T(128)}) custom-call(s32[1]{0:T(128)} %bitcast.c_ref, bf16[512,256]{1,0:T(8,128)(2,1)} %get-tuple-element.28.bc_ref, bf16[512,2560]{1,0:T(8,128)(2,1)} %x_ref.5, bf16[512,2560]{1,0:T(8,128)(2,1)} %dy_ref.5, ...), custom_call_target="tpu_custom_call" | custom-call | flops 20000000000 | bytes 16000000 | tf_op jit(solution)/shard_map/pairs/pallas_call | solution.py:337
  42.7 8.8 %all-to-all-done.in_ref = f32[64,48,128]{2,1,0:T(8,128)S(1)} async-done(((f32[64,48,128]{2,1,0:T(8,128)}), f32[64,48,128]{2,1,0:T(8,128)S(1)}, u32[]{:S(2)}, u32[]{:S(2)}) %all-to-all-start) | async-done | bytes 1572896 | tf_op jit(solution)/shard_map/all_to_all | solution.py:670
  51.5 1.9 %scan_chips.1 = f32[64,40,128]{2,1,0:T(8,128)} custom-call(s32[1]{0:T(128)} %bitcast.c_ref, f32[64,48,128]{2,1,0:T(8,128)S(1)} %all-to-all-done.in_ref, s32[1]{0:T(128)} %get-tuple-element.34.after_ref), custom_call_target="tpu_custom_call" | custom-call | tf_op jit(solution)/shard_map/scan_chips/pallas_call | solution.py:245
  53.4 5.5 %all-to-all-start.1 = ((f32[64,40,128]{2,1,0:T(8,128)}), f32[64,40,128]{2,1,0:T(8,128)S(1)}, u32[]{:S(2)}, u32[]{:S(2)}) async-start(f32[64,40,128]{2,1,0:T(8,128)} %scan_chips.1), calls=%async_computation.1 | async-start | bytes 2621440 | tf_op jit(solution)/shard_map/all_to_all | solution.py:670
  59.0 2.4 %collective-permute-start.2 = (f32[64,48,128]{2,1,0:T(8,128)}, f32[64,48,128]{2,1,0:T(8,128)S(1)}, u32[]{:S(2)}, u32[]{:S(2)}) collective-permute-start(f32[64,48,128]{2,1,0:T(8,128)} %get-tuple-element.31.mine_ref), channel_id=1, source_target_pairs={{0,1},{1,0},{2,3},{3,2},{4,5},{5,4},{6,7},{7,6},{8,9},{9,8},{10,11... | collective-permute-start | bytes 4718600 | tf_op jit(solution)/shard_map/ppermute | solution.py:666
  61.4 16.3 %all-to-all-done.1.came_ref = f32[64,40,128]{2,1,0:T(8,128)S(1)} async-done(((f32[64,40,128]{2,1,0:T(8,128)}), f32[64,40,128]{2,1,0:T(8,128)S(1)}, u32[]{:S(2)}, u32[]{:S(2)}) %all-to-all-start.1) | async-done | bytes 1310752 | tf_op jit(solution)/shard_map/all_to_all | solution.py:670
  77.7 3.7 %collective-permute-start.1 = (f32[64,40,128]{2,1,0:T(8,128)S(1)}, f32[64,40,128]{2,1,0:T(8,128)S(1)}, u32[]{:S(2)}, u32[]{:S(2)}) collective-permute-start(f32[64,40,128]{2,1,0:T(8,128)S(1)} %all-to-all-done.1.came_ref), channel_id=1, source_target_pairs={{0,1},{1,0},{2,3},{3,2},{4,5},{5,4},{6,7},{7,6},{8,9},{9,8},{10,11... | collective-permute-start | bytes 3932168 | tf_op jit(solution)/shard_map/ppermute | solution.py:666
  81.3 0.0 copy-start
  81.4 1.7 %copy-done = bf16[512,2560]{1,0:T(8,128)(2,1)S(1)} copy-done((bf16[512,2560]{1,0:T(8,128)(2,1)S(1)}, bf16[512,2560]{1,0:T(8,128)(2,1)}, u32[]{:S(2)}) %copy-start) | copy-done | bytes 2621464
  83.1 0.0 copy-start.1
  83.1 0.0 copy-start.3
  83.1 0.9 carry.1
  84.0 0.0 copy-start.4
  84.0 0.0 collective-permute-done.2.theirs_ref
  84.0 0.0 collective-permute-done.1.came_ref
  84.0 0.8 copy-done.1
  84.8 0.2 copy-done.3
  85.0 3.7 %weight_part.1 = (f32[2,1280,128]{2,1,0:T(8,128)S(1)}, f32[2,1280,128]{2,1,0:T(8,128)S(1)}, bf16[128,2560]{1,0:T(8,128)(2,1)S(1)}) custom-call(s32[1]{0:T(128)} %bitcast.c_ref, f32[512,128]{1,0:T(8,128)S(1)} %get-tuple-element.36.accmine_ref, bf16[512,2560]{1,0:T(8,128)(2,1)S(1)} %copy-done.1, f32[64,40,128]{2,1,0:T(8,128)S(1)} %collective-permute-done.1.came_ref, ...), custom_call_target="tpu_custom_call" | custom-call | flops 2000000000 | bytes 12000000 | tf_op jit(solution)/shard_map/weight_part/pallas_call | solution.py:450
  88.7 0.0 copy-done.4
  88.7 0.0 copy-start.5
  88.7 0.1 collective-permute-start.3
  88.8 3.0 %collective-permute-done.3.b_ref = f32[2,1280,128]{2,1,0:T(8,128)S(1)} collective-permute-done((f32[2,1280,128]{2,1,0:T(8,128)S(1)}, f32[2,1280,128]{2,1,0:T(8,128)S(1)}, u32[]{:S(2)}, u32[]{:S(2)}) %collective-permute-start.3) | collective-permute-done | bytes 1310752 | tf_op jit(solution)/shard_map/ppermute | solution.py:666
  91.8 1.1 pair_add.1.refs_0_
  92.9 0.0 copy-done.5
  93.0 0.0 copy-start.6
  93.0 4.7 %all-to-all-start.2 = ((f32[64,40,128]{2,1,0:T(8,128)}), f32[64,40,128]{2,1,0:T(8,128)S(1)}, u32[]{:S(2)}, u32[]{:S(2)}) async-start(f32[64,40,128]{2,1,0:T(8,128)} %bitcast.2), calls=%async_computation.2 | async-start | bytes 2621440 | tf_op jit(solution)/shard_map/all_to_all | solution.py:670
  97.7 0.0 copy-done.6
  97.7 0.1 broadcast_in_dim.7
  97.8 0.7 broadcast_in_dim_reshape.3.skip_ref
  98.5 10.8 %outputs.2 = (bf16[512,2560]{1,0:T(8,128)(2,1)}, bf16[512,2560]{1,0:T(8,128)(2,1)}, s32[1]{0:T(128)}) custom-call(s32[1]{0:T(128)} %bitcast.c_ref, bf16[512,256]{1,0:T(8,128)(2,1)} %get-tuple-element.28.bc_ref, bf16[512,2560]{1,0:T(8,128)(2,1)} %x_ref.5, bf16[512,2560]{1,0:T(8,128)(2,1)} %dy_ref.5, f32[4,16,512]{2,1,0:T(8,128)} %get-tuple-element.29.cum_ref, ...), custom_call_target="tpu_custom_call" | custom-call | flops 12000000000 | bytes 7000000 | tf_op jit(solution)/shard_map/outputs/pallas_call | solution.py:527
  109.3 8.9 %all-to-all-done.2.in_ref = f32[64,40,128]{2,1,0:T(8,128)S(1)} async-done(((f32[64,40,128]{2,1,0:T(8,128)}), f32[64,40,128]{2,1,0:T(8,128)S(1)}, u32[]{:S(2)}, u32[]{:S(2)}) %all-to-all-start.2) | async-done | bytes 1310752 | tf_op jit(solution)/shard_map/all_to_all | solution.py:670
  118.2 2.4 %chip_total.1 = (f32[64,40,128]{2,1,0:T(8,128)}, s32[1]{0:T(128)}) custom-call(s32[1]{0:T(128)} %get-tuple-element.43.c_ref, f32[64,40,128]{2,1,0:T(8,128)S(1)} %all-to-all-done.2.in_ref), custom_call_target="tpu_custom_call" | custom-call | tf_op jit(solution)/shard_map/chip_total/pallas_call | solution.py:610
  120.6 5.6 %all-to-all-start.3 = ((f32[64,40,128]{2,1,0:T(8,128)}), f32[64,40,128]{2,1,0:T(8,128)S(1)}, u32[]{:S(2)}, u32[]{:S(2)}) async-start(f32[64,40,128]{2,1,0:T(8,128)} %get-tuple-element.50), calls=%async_computation.3 | async-start | bytes 2621440 | tf_op jit(solution)/shard_map/all_to_all | solution.py:670
  126.2 11.5 %outputs.3 = (bf16[512,2560]{1,0:T(8,128)(2,1)}, bf16[512,2560]{1,0:T(8,128)(2,1)}, s32[1]{0:T(128)}) custom-call(s32[1]{0:T(128)} %get-tuple-element.44.c_ref, bf16[512,256]{1,0:T(8,128)(2,1)} %get-tuple-element.28.bc_ref, bf16[512,2560]{1,0:T(8,128)(2,1)} %x_ref.5, bf16[512,2560]{1,0:T(8,128)(2,1)} %dy_ref.5, ...), custom_call_target="tpu_custom_call", output_to_operand_aliasing={{0}: (9, {}), {1}: (10, {})} | custom-call | flops 12000000000 | bytes 7000000 | tf_op jit(solution)/shard_map/outputs/pallas_call | solution.py:527
  137.7 7.2 %all-to-all-done.3 = f32[64,40,128]{2,1,0:T(8,128)S(1)} async-done(((f32[64,40,128]{2,1,0:T(8,128)}), f32[64,40,128]{2,1,0:T(8,128)S(1)}, u32[]{:S(2)}, u32[]{:S(2)}) %all-to-all-start.3) | async-done | bytes 1310752 | tf_op jit(solution)/shard_map/all_to_all | solution.py:670
  144.9 1.2 hold.1
  146.1 3.6 %collective-permute-start.4 = (f32[2,1280,128]{2,1,0:T(8,128)S(1)}, f32[2,1280,128]{2,1,0:T(8,128)S(1)}, u32[]{:S(2)}, u32[]{:S(2)}) collective-permute-start(f32[2,1280,128]{2,1,0:T(8,128)S(1)} %get-tuple-element.51.half_ref), channel_id=1, source_target_pairs={{0,1},{1,0},{2,3},{3,2},{4,5},{5,4},{6,7},{7,6},{8,9},{9,8},{10,11... | collective-permute-start | bytes 3932168 | tf_op jit(solution)/shard_map/ppermute | solution.py:666
  149.7 1.8 %place.2.refs_0_ = f32[2560,256]{1,0:T(8,128)} custom-call(s32[1]{0:T(128)} %get-tuple-element.52.c_ref, f32[2,1280,128]{2,1,0:T(8,128)S(1)} %get-tuple-element.51.half_ref), custom_call_target="tpu_custom_call" | custom-call | tf_op jit(solution)/shard_map/place/pallas_call | solution.py:649
  151.5 0.8 collective-permute-done.4.half_ref
  152.3 1.2 place.3
Async XLA Ops:
  10.0 4.8 %collective-permute-start = (f32[64,48,128]{2,1,0:T(8,128)}, f32[64,48,128]{2,1,0:T(8,128)S(1)}, u32[]{:S(2)}, u32[]{:S(2)}) collective-permute-start(f32[64,48,128]{2,1,0:T(8,128)} %get-tuple-element.32), channel_id=1, source_target_pairs={{0,1},{1,0},{2,3},{3,2},{4,5},{5,4},{6,7},{7,6},{8,9},{9,8},{10,11... | collective-permute-start | bytes 4718600 | tf_op jit(solution)/shard_map/ppermute | solution.py:666
  14.7 1.4 copy-start.2
  17.5 34.0 %all-to-all-start = ((f32[64,48,128]{2,1,0:T(8,128)}), f32[64,48,128]{2,1,0:T(8,128)S(1)}, u32[]{:S(2)}, u32[]{:S(2)}) async-start(f32[64,48,128]{2,1,0:T(8,128)} %chip_sum.1.after_ref), calls=%async_computation | async-start | bytes 3145728 | tf_op jit(solution)/shard_map/all_to_all | solution.py:670
  53.4 24.3 %all-to-all-start.1 = ((f32[64,40,128]{2,1,0:T(8,128)}), f32[64,40,128]{2,1,0:T(8,128)S(1)}, u32[]{:S(2)}, u32[]{:S(2)}) async-start(f32[64,40,128]{2,1,0:T(8,128)} %scan_chips.1), calls=%async_computation.1 | async-start | bytes 2621440 | tf_op jit(solution)/shard_map/all_to_all | solution.py:670
  59.0 25.0 %collective-permute-start.2 = (f32[64,48,128]{2,1,0:T(8,128)}, f32[64,48,128]{2,1,0:T(8,128)S(1)}, u32[]{:S(2)}, u32[]{:S(2)}) collective-permute-start(f32[64,48,128]{2,1,0:T(8,128)} %get-tuple-element.31.mine_ref), channel_id=1, source_target_pairs={{0,1},{1,0},{2,3},{3,2},{4,5},{5,4},{6,7},{7,6},{8,9},{9,8},{10,11... | collective-permute-start | bytes 4718600 | tf_op jit(solution)/shard_map/ppermute | solution.py:666
  77.7 6.3 %collective-permute-start.1 = (f32[64,40,128]{2,1,0:T(8,128)S(1)}, f32[64,40,128]{2,1,0:T(8,128)S(1)}, u32[]{:S(2)}, u32[]{:S(2)}) collective-permute-start(f32[64,40,128]{2,1,0:T(8,128)S(1)} %all-to-all-done.1.came_ref), channel_id=1, source_target_pairs={{0,1},{1,0},{2,3},{3,2},{4,5},{5,4},{6,7},{7,6},{8,9},{9,8},{10,11... | collective-permute-start | bytes 3932168 | tf_op jit(solution)/shard_map/ppermute | solution.py:666
  81.3 1.7 %copy-start = (bf16[512,2560]{1,0:T(8,128)(2,1)S(1)}, bf16[512,2560]{1,0:T(8,128)(2,1)}, u32[]{:S(2)}) copy-start(bf16[512,2560]{1,0:T(8,128)(2,1)} %get-tuple-element.33.w_ref) | copy-start | bytes 7864324
  83.1 1.7 %copy-start.1 = (bf16[512,2560]{1,0:T(8,128)(2,1)S(1)}, bf16[512,2560]{1,0:T(8,128)(2,1)}, u32[]{:S(2)}) copy-start(bf16[512,2560]{1,0:T(8,128)(2,1)} %get-tuple-element.37.wother_ref) | copy-start | bytes 7864324
  83.1 1.9 %copy-start.3 = (f32[512,256]{1,0:T(8,128)S(1)}, f32[512,256]{1,0:T(8,128)}, u32[]{:S(2)}) copy-start(f32[512,256]{1,0:T(8,128)} %get-tuple-element.38.dbc_ref) | copy-start | bytes 1572868
  84.0 4.7 %copy-start.4 = (bf16[128,2560]{1,0:T(8,128)(2,1)}, bf16[128,2560]{1,0:T(8,128)(2,1)S(1)}, u32[]{:S(2)}) copy-start(bf16[128,2560]{1,0:T(8,128)(2,1)S(1)} %get-tuple-element.35.smine_ref) | copy-start | bytes 1966084
  88.7 4.2 %copy-start.5 = (bf16[128,2560]{1,0:T(8,128)(2,1)}, bf16[128,2560]{1,0:T(8,128)(2,1)S(1)}, u32[]{:S(2)}) copy-start(bf16[128,2560]{1,0:T(8,128)(2,1)S(1)} %get-tuple-element.40.sother_ref) | copy-start | bytes 1966084
  88.7 3.1 %collective-permute-start.3 = (f32[2,1280,128]{2,1,0:T(8,128)S(1)}, f32[2,1280,128]{2,1,0:T(8,128)S(1)}, u32[]{:S(2)}, u32[]{:S(2)}) collective-permute-start(f32[2,1280,128]{2,1,0:T(8,128)S(1)} %get-tuple-element.42), channel_id=1, source_target_pairs={{0,1},{1,0},{2,3},{3,2},{4,5},{5,4},{6,7},{7,6},{8,9},{9,8},{10,11... | collective-permute-start | bytes 3932168 | tf_op jit(solution)/shard_map/ppermute | solution.py:666
  93.0 4.8 %copy-start.6 = (f32[40]{0:T(128)S(1)}, f32[40]{0:T(128)}, u32[]{:S(2)}) copy-start(f32[40]{0:T(128)} %param.12) | copy-start | bytes 484
  93.0 25.2 %all-to-all-start.2 = ((f32[64,40,128]{2,1,0:T(8,128)}), f32[64,40,128]{2,1,0:T(8,128)S(1)}, u32[]{:S(2)}, u32[]{:S(2)}) async-start(f32[64,40,128]{2,1,0:T(8,128)} %bitcast.2), calls=%async_computation.2 | async-start | bytes 2621440 | tf_op jit(solution)/shard_map/all_to_all | solution.py:670
  120.6 24.3 %all-to-all-start.3 = ((f32[64,40,128]{2,1,0:T(8,128)}), f32[64,40,128]{2,1,0:T(8,128)S(1)}, u32[]{:S(2)}, u32[]{:S(2)}) async-start(f32[64,40,128]{2,1,0:T(8,128)} %get-tuple-element.50), calls=%async_computation.3 | async-start | bytes 2621440 | tf_op jit(solution)/shard_map/all_to_all | solution.py:670
  146.1 6.2 %collective-permute-start.4 = (f32[2,1280,128]{2,1,0:T(8,128)S(1)}, f32[2,1280,128]{2,1,0:T(8,128)S(1)}, u32[]{:S(2)}, u32[]{:S(2)}) collective-permute-start(f32[2,1280,128]{2,1,0:T(8,128)S(1)} %get-tuple-element.51.half_ref), channel_id=1, source_target_pairs={{0,1},{1,0},{2,3},{3,2},{4,5},{5,4},{6,7},{7,6},{8,9},{9,8},{10,11... | collective-permute-start | bytes 3932168 | tf_op jit(solution)/shard_map/ppermute | solution.py:666
